TPU v7x, 128 devices: a whole 4x4x4 slice. The times are simulated.
128 devices in a mesh: stream: 16 (over x_lo, z, core), span: 8 (over y, x_hi).
Axes of the slice: x: 4 (x_hi: 2, x_lo: 2; x = x_hi * 2 + x_lo), y: 4, z: 4, core: 2. Of those that a mesh axis runs over, the one named last changes fastest.
Arguments:
- main_flow: float32 [3, 192, 256, 1024], P(None, 'stream', 'span'), may hold values from -6 to 6
- precursor: float32 [3, 256, 256, 1024], P(None, 'stream', 'span'), may hold values from -6 to 6
- magnet_field: float32 [3, 192, 256, 1024], P(None, 'stream', 'span'), may hold values from -6 to 6
- inlet_rows: int32 [256], replicated, may hold values from 0 to 255, each once
Outputs:
- main_next: float32 [3, 192, 256, 1024], P(None, 'stream', 'span')
- precursor_next: float32 [3, 256, 256, 1024], P(None, 'stream', 'span')
Inputs may be any that keep to these rules, and one draw needn't show every extreme that they name: `inlet_rows`: a permutation of the spanwise rows.
All inputs are finite; a program needn't handle non-finite values.
Results may differ from a plain program's by a relative error of at most 0.0001.
Values sent between devices are 32-bit elements; how exact they have to be, the bound alone decides.
No kernel may reach another device: no remote copies, remote signals or barrier semaphores. Data moves between devices by JAX's collectives and lax.ppermute only.
A program may use at most 128 MiB of HBM per device.

v0:
```python
import functools

import jax
import jax.numpy as jnp
from jax import lax
from jax.experimental import pallas as pl
from jax.experimental.pallas import tpu as pltpu
from jax.sharding import PartitionSpec as P

TIME_STEP = 0.1
VISCOSITY = 0.02
SMAGORINSKY = 0.03
INTERACTION = 0.5

LANES = 128
SUBLANES = 8
VMEM_LIMIT = 56 << 20
SMALL = pl.CostEstimate(flops=1, bytes_accessed=1, transcendentals=0)
F32 = jnp.float32
ANY = pl.BlockSpec(memory_space=pl.ANY)
HBM = pl.BlockSpec(memory_space=pltpu.HBM)
VMEM = pl.BlockSpec(memory_space=pltpu.VMEM)
SMEM = pl.BlockSpec(memory_space=pltpu.SMEM)

EDDY_SCALE = (TIME_STEP * SMAGORINSKY) ** 2 / 4.0
EDDY_FLOOR = (TIME_STEP * SMAGORINSKY) ** 2 * 1e-06


def update(u, forward, backward, magnet):
    diff = [[forward[j][i] - backward[j][i] for j in range(3)] for i in range(3)]
    diag = diff[0][0] * diff[0][0] + diff[1][1] * diff[1][1] + diff[2][2] * diff[2][2]
    quad = diag + diag
    for i, j in ((0, 1), (0, 2), (1, 2)):
        pair = diff[i][j] + diff[j][i]
        quad = quad + pair * pair
    square = quad * EDDY_SCALE + EDDY_FLOOR
    eddy = square * lax.rsqrt(square)
    visc = eddy + TIME_STEP * VISCOSITY
    keep = (1.0 - 6.0 * TIME_STEP * VISCOSITY) - 6.0 * eddy
    if magnet is not None:
        scale = TIME_STEP * INTERACTION
        aligned = (u[0] * magnet[0] + u[1] * magnet[1] + u[2] * magnet[2]) * scale
        strength = magnet[0] * magnet[0] + magnet[1] * magnet[1] + magnet[2] * magnet[2]
        keep = keep - strength * scale
    speed = [u[j] * (-0.5 * TIME_STEP) for j in range(3)]
    out = []
    for i in range(3):
        around = (forward[0][i] + backward[0][i]) + (forward[1][i] + backward[1][i])
        around = around + (forward[2][i] + backward[2][i])
        value = keep * u[i] + visc * around
        value = value + speed[0] * diff[i][0] + speed[1] * diff[i][1] + speed[2] * diff[i][2]
        if magnet is not None:
            value = value + aligned * magnet[i]
        out.append(value)
    return out


def shifted_lanes(read, tiles):
    shape = (SUBLANES, LANES)
    lane = lax.broadcasted_iota(jnp.int32, shape, 1)
    zero = jnp.zeros(shape, F32)
    here = read(0)
    left = zero
    ahead = pltpu.roll(here, LANES - 1, 1)
    for t in range(tiles):
        behind = pltpu.roll(here, 1, 1)
        following = read(t + 1) if t + 1 < tiles else None
        right = pltpu.roll(following, LANES - 1, 1) if t + 1 < tiles else zero
        yield here, jnp.where(lane == LANES - 1, right, ahead), jnp.where(lane == 0, left, behind)
        here, left, ahead = following, behind, right


def plane_rows(flow, before, x, after, at, magnet, store):
    tiles = flow.shape[2]
    streams = [
        shifted_lanes(lambda t, c=c: flow[c, x, t, pl.ds(at, SUBLANES), :], tiles) for c in range(3)
    ]
    for t in range(tiles):
        along = [next(stream) for stream in streams]
        u = [value[0] for value in along]
        forward = [
            [flow[c, after, t, pl.ds(at, SUBLANES), :] for c in range(3)],
            [flow[c, x, t, pl.ds(at + 1, SUBLANES), :] for c in range(3)],
            [value[1] for value in along],
        ]
        backward = [
            [flow[c, before, t, pl.ds(at, SUBLANES), :] for c in range(3)],
            [flow[c, x, t, pl.ds(at - 1, SUBLANES), :] for c in range(3)],
            [value[2] for value in along],
        ]
        field = None if magnet is None else [magnet(c, t) for c in range(3)]
        for c, value in enumerate(update(u, forward, backward, field)):
            store(c, t, value)


def tile_of(t):
    return pl.ds(t * LANES, LANES)


def place():
    span, stream = lax.axis_index("span"), lax.axis_index("stream")
    return span == 0, span == lax.axis_size("span") - 1, stream == 0, stream == lax.axis_size("stream") - 1


def copy_planes(source, first, count, flow, i, sem):
    for t in range(flow.shape[2]):
        pltpu.make_async_copy(
            source.at[:, pl.ds(first, count), :, tile_of(t)],
            flow.at[:, pl.ds(i, count), t, pl.ds(BASE, source.shape[2])],
            sem,
        ).start()


def wait_planes(flow, count, rows, sem):
    part = flow.at[:, pl.ds(0, count), :, pl.ds(BASE, rows)]
    pltpu.make_async_copy(part, part, sem).wait()


BASE = SUBLANES
GROUP = 4


def copy_halos(low, high, flow, i, first, count, rows, sem):
    walls = place()
    for n, (ref, at) in enumerate(((low, BASE - 1), (high, BASE + rows))):

        @pl.when(jnp.logical_not(walls[n]))
        def _(n=n, ref=ref, at=at):
            for t in range(flow.shape[2]):
                pltpu.make_async_copy(
                    ref.at[:, pl.ds(first, count), :, tile_of(t)],
                    flow.at[:, pl.ds(i, count), t, pl.ds(at, 1)],
                    sem.at[n],
                ).start()

        @pl.when(walls[n])
        def _(at=at):
            for c in range(3):
                for x in range(count):
                    for t in range(flow.shape[2]):
                        flow[c, i + x, t, pl.ds(at, 1), :] = jnp.zeros((1, LANES), F32)


def wait_halos(flow, i, count, rows, sem):
    walls = place()
    for n, at in enumerate((BASE - 1, BASE + rows)):

        @pl.when(jnp.logical_not(walls[n]))
        def _(n=n, at=at):
            part = flow.at[:, pl.ds(i, count), :, pl.ds(at, 1)]
            pltpu.make_async_copy(part, part, sem.at[n]).wait()


def interior_kernel(edges, n_main, n_prec, rows, *refs):
    if edges:
        main, prec, magnet, low, high, _, _, main_out, prec_out = refs[:9]
        flow, field, result, in_sem, field_sem, out_sem, halo_sem = refs[9:]
    else:
        main, prec, magnet, main_out, prec_out, token = refs[:6]
        flow, field, result, in_sem, field_sem, out_sem = refs[6:]
        token[...] = jnp.zeros_like(token)
    total = n_main + n_prec
    last = rows // SUBLANES - 1
    kept = [0, last] if edges else list(range(1, last))
    if edges:
        spans = [(0, 0, SUBLANES), (SUBLANES, last * SUBLANES, SUBLANES)]
    else:
        spans = [(0, SUBLANES, (last - 1) * SUBLANES)]

    if edges:
        copy_halos(low, high, flow, 0, 0, total, rows, halo_sem)
    for g in range(n_prec // GROUP):
        copy_planes(prec, g * GROUP, GROUP, flow, g * GROUP, in_sem.at[g])
    for g in range(n_main // GROUP):
        copy_planes(main, g * GROUP, GROUP, flow, n_prec + g * GROUP, in_sem.at[n_prec // GROUP + g])
        planes = pl.ds(g * GROUP, GROUP)
        for at, row, size in spans:
            pltpu.make_async_copy(
                magnet.at[:, planes, pl.ds(row, size)], field.at[:, planes, pl.ds(at, size)], field_sem.at[g]
            ).start()

    def stores(target, x, i):
        return [
            pltpu.make_async_copy(
                result.at[:, i, pl.ds(at, size)], target.at[:, x, pl.ds(row, size)], out_sem.at[i]
            )
            for at, row, size in spans
        ]

    def run(target, x, i, with_field):
        for n, k in enumerate(kept):
            part = pl.ds(n * SUBLANES, SUBLANES)

            def store(c, t, value, part=part):
                result[c, i, part, tile_of(t)] = value

            def read(c, t, part=part):
                return field[c, x, part, tile_of(t)]

            at = BASE + k * SUBLANES
            plane_rows(flow, i - 1, i, i + 1, at, read if with_field else None, store)
        for copy in stores(target, x, i):
            copy.start()

    def wait_field(g):
        part = field.at[:, pl.ds(0, GROUP)]
        pltpu.make_async_copy(part, part, field_sem.at[g]).wait()

    if edges:
        wait_halos(flow, 0, total, rows, halo_sem)
    wait_planes(flow, GROUP, rows, in_sem.at[0])

    def prec_step(x, carry):
        @pl.when((x + 1) % GROUP == 0)
        def _():
            wait_planes(flow, GROUP, rows, in_sem.at[(x + 1) // GROUP])

        run(prec_out, x, x, False)
        return carry

    lax.fori_loop(1, n_prec - 1, prec_step, 0)
    wait_planes(flow, GROUP, rows, in_sem.at[n_prec // GROUP])
    wait_field(0)

    def main_step(x, carry):
        @pl.when((x + 1) % GROUP == 0)
        def _():
            g = (x + 1) // GROUP
            wait_planes(flow, GROUP, rows, in_sem.at[n_prec // GROUP + g])
            wait_field(g)

        run(main_out, x, n_prec + x, True)
        return carry

    lax.fori_loop(1, n_main - 1, main_step, 0)

    def drain(i, carry):
        part = result.at[:, 0]
        pltpu.make_async_copy(part, part, out_sem.at[i]).wait()
        return carry

    lax.fori_loop(1, n_prec - 1, drain, 0)
    lax.fori_loop(n_prec + 1, total - 1, drain, 0)


def interior(edges, main, prec, magnet, extra=()):
    _, n_main, rows, depth = main.shape
    n_prec = prec.shape[1]
    total = n_main + n_prec
    kept = 2 * SUBLANES if edges else rows - 2 * SUBLANES
    scratch = [
        pltpu.VMEM((3, total, depth // LANES, rows + 2 * SUBLANES, LANES), F32),
        pltpu.VMEM((3, n_main, kept, depth), F32),
        pltpu.VMEM((3, total, kept, depth), F32),
        pltpu.SemaphoreType.DMA((total // GROUP,)),
        pltpu.SemaphoreType.DMA((n_main // GROUP,)),
        pltpu.SemaphoreType.DMA((total,)),
    ]
    outs = [jax.ShapeDtypeStruct(main.shape, F32), jax.ShapeDtypeStruct(prec.shape, F32)]
    out_specs = [HBM, HBM]
    if edges:
        scratch += [pltpu.SemaphoreType.DMA((2,))]
        low, high, main_out, prec_out = extra
        operands = (main, prec, magnet, low, high, main_out, prec_out)
        specs = [HBM] * 3 + [ANY] * 2 + [HBM] * 2
        aliases = {5: 0, 6: 1}
    else:
        operands = (main, prec, magnet)
        specs = [HBM] * 3
        aliases = {}
        outs.append(jax.ShapeDtypeStruct((SUBLANES, LANES), F32))
        out_specs.append(VMEM)
    return pl.pallas_call(
        functools.partial(interior_kernel, edges, n_main, n_prec, rows),
        out_shape=outs,
        in_specs=specs,
        out_specs=out_specs,
        scratch_shapes=scratch,
        input_output_aliases=aliases,
        compiler_params=pltpu.CompilerParams(vmem_limit_bytes=VMEM_LIMIT),
        cost_estimate=SMALL,
        name="edge_rows" if edges else "inner_rows",
    )(*operands)


def boundary_kernel(n_main, n_prec, rows, jobs, chunks, *refs):
    main, prec, magnet, low, high, before, after = refs[:7]
    slots = refs[7 : 7 + chunks]
    main_out, prec_out = refs[9 + chunks : 11 + chunks]
    flow, field, result, sem, side_sem, out_sem, halo_sem, field_sem = refs[11 + chunks :]
    last = rows // SUBLANES - 1
    tiles = flow.shape[2]
    _, _, at_inlet, at_outlet = place()
    half = lax.axis_index("span") % 2

    def fill(source, first, job, at):
        copy_planes(source, first, 1, flow, 3 * job + at, side_sem.at[job])

    for job, (is_main, at_low) in enumerate(jobs):
        source = main if is_main else prec
        count = n_main if is_main else n_prec
        kind = 0 if is_main else 1
        x = 0 if at_low else count - 1
        if at_low:
            copy_planes(source, 0, 2, flow, 3 * job + 1, sem.at[job])
        else:
            copy_planes(source, count - 2, 2, flow, 3 * job, sem.at[job])
        if is_main:
            pltpu.make_async_copy(magnet.at[:, x], field.at[:, job], field_sem.at[job]).start()
        copy_halos(low, high, flow, 3 * job + 1, n_prec + x if is_main else x, 1, rows, halo_sem.at[job])
        if at_low and is_main:

            @pl.when(at_inlet)
            def _(job=job):
                for k in range(chunks):
                    begin = jnp.bitwise_xor(half, k) * (tiles // chunks)
                    for t in range(tiles // chunks):
                        pltpu.make_async_copy(
                            slots[k].at[:, :, tile_of(t)],
                            flow.at[:, 3 * job, begin + t, pl.ds(BASE, rows)],
                            side_sem.at[job],
                        ).start()

            @pl.when(jnp.logical_not(at_inlet))
            def _(job=job, kind=kind):
                fill(before, kind, job, 0)

        elif at_low:
            fill(before, kind, job, 0)
        elif is_main:

            @pl.when(at_outlet)
            def _(job=job, source=source, x=x):
                fill(source, x, job, 2)

            @pl.when(jnp.logical_not(at_outlet))
            def _(job=job, kind=kind):
                fill(after, kind, job, 2)

        else:
            fill(after, kind, job, 2)
    for job, (is_main, at_low) in enumerate(jobs):
        x = 0 if at_low else (n_main if is_main else n_prec) - 1
        middle = 3 * job + 1
        wait_planes(flow, 2, rows, sem.at[job])
        wait_planes(flow, 1, rows, side_sem.at[job])
        wait_halos(flow, middle, 1, rows, halo_sem.at[job])
        if is_main:
            pltpu.make_async_copy(field.at[:, job], field.at[:, job], field_sem.at[job]).wait()

        def step(k, carry, job=job, middle=middle, is_main=is_main):
            part = pl.ds(pl.multiple_of(k * SUBLANES, SUBLANES), SUBLANES)

            def store(c, t, value):
                result[c, job, part, tile_of(t)] = value

            def read(c, t):
                return field[c, job, part, tile_of(t)]

            at = BASE + k * SUBLANES
            plane_rows(flow, middle - 1, middle, middle + 1, at, read if is_main else None, store)
            return carry

        lax.fori_loop(0, last + 1, step, 0, unroll=2)
        target = main_out if is_main else prec_out
        pltpu.make_async_copy(result.at[:, job], target.at[:, x], out_sem.at[job]).start()
    for job, (is_main, at_low) in enumerate(jobs):
        pltpu.make_async_copy(result.at[:, job], main_out.at[:, 0], out_sem.at[job]).wait()


def boundary(jobs, main, prec, magnet, low, high, before, after, slots, main_out, prec_out):
    _, n_main, rows, depth = main.shape
    n_prec = prec.shape[1]
    count = len(jobs)
    return pl.pallas_call(
        functools.partial(boundary_kernel, n_main, n_prec, rows, jobs, len(slots)),
        out_shape=[jax.ShapeDtypeStruct(main.shape, F32), jax.ShapeDtypeStruct(prec.shape, F32)],
        in_specs=[HBM] * 3 + [ANY] * (4 + len(slots)) + [HBM] * 2,
        out_specs=[HBM, HBM],
        scratch_shapes=[
            pltpu.VMEM((3, 3 * count, depth // LANES, rows + 2 * SUBLANES, LANES), F32),
            pltpu.VMEM((3, count, rows, depth), F32),
            pltpu.VMEM((3, count, rows, depth), F32),
            pltpu.SemaphoreType.DMA((count,)),
            pltpu.SemaphoreType.DMA((count,)),
            pltpu.SemaphoreType.DMA((count,)),
            pltpu.SemaphoreType.DMA((count, 2)),
            pltpu.SemaphoreType.DMA((count,)),
        ],
        input_output_aliases={7 + len(slots): 0, 8 + len(slots): 1},
        compiler_params=pltpu.CompilerParams(vmem_limit_bytes=VMEM_LIMIT),
        cost_estimate=SMALL,
        name="end_planes" if count > 1 else "inlet_plane",
    )(main, prec, magnet, low, high, before, after, *slots, main_out, prec_out)


def pack_kernel(n_main, n_prec, rows, depth, *refs):
    main, prec, row_low, row_high, face_low, face_high, kept, given, low_tile, high_tile, sem, row_sem = refs
    half = lax.axis_index("span") % 2
    width = depth // 2
    own = pl.ds(pl.multiple_of(half * width, width), width)
    other = pl.ds(pl.multiple_of((1 - half) * width, width), width)
    first, last = pl.ds(0, SUBLANES), pl.ds(rows - SUBLANES, SUBLANES)
    groups = [(prec, g, g) for g in range(0, n_prec, GROUP)] + [(main, g, n_prec + g) for g in range(0, n_main, GROUP)]
    row_copies = []
    for n, (source, x, i) in enumerate(groups):
        for m, (part, target) in enumerate(((first, low_tile), (last, high_tile))):
            row_copies.append(
                pltpu.make_async_copy(
                    source.at[:, pl.ds(x, GROUP), part], target.at[:, pl.ds(i, GROUP)], row_sem.at[2 * n + m]
                )
            )
    pairs = [
        (prec.at[:, n_prec - 1, :, other], given),
        (prec.at[:, n_prec - 1, :, own], kept),
    ]
    for source, kind, count in ((main, 0, n_main), (prec, 1, n_prec)):
        pairs.append((source.at[:, count - 1], face_high.at[:, kind]))
        pairs.append((source.at[:, 0], face_low.at[:, kind]))
    copies = [pltpu.make_async_copy(a, b, sem.at[n]) for n, (a, b) in enumerate(pairs)]
    for copy in row_copies + copies:
        copy.start()
    for n, (_, _, i) in enumerate(groups):
        row_copies[2 * n].wait()
        row_copies[2 * n + 1].wait()
        for c in range(3):
            for x in range(i, i + GROUP):
                row_low[c, x] = low_tile[c, x, pl.ds(0, 1), :]
                row_high[c, x] = high_tile[c, x, pl.ds(SUBLANES - 1, 1), :]
    for copy in copies:
        copy.wait()


def pack(main, prec):
    _, n_main, rows, depth = main.shape
    n_prec = prec.shape[1]
    total = n_main + n_prec
    face = jax.ShapeDtypeStruct((3, 2, rows, depth), F32)
    packed = jax.ShapeDtypeStruct((3, total, 1, depth), F32)
    part = jax.ShapeDtypeStruct((3, rows, depth // 2), F32)
    return pl.pallas_call(
        functools.partial(pack_kernel, n_main, n_prec, rows, depth),
        out_shape=[packed, packed, face, face, part, part],
        in_specs=[HBM, HBM],
        out_specs=[VMEM] * 6,
        scratch_shapes=[
            pltpu.VMEM((3, total, SUBLANES, depth), F32),
            pltpu.VMEM((3, total, SUBLANES, depth), F32),
            pltpu.SemaphoreType.DMA((6,)),
            pltpu.SemaphoreType.DMA((2 * total // GROUP,)),
        ],
        compiler_params=pltpu.CompilerParams(vmem_limit_bytes=VMEM_LIMIT),
        cost_estimate=SMALL,
        name="pack_halos",
    )(main, prec)


def join_kernel(kept, arrived, out, sem):
    @pl.when(place()[3])
    def _():
        copies = [pltpu.make_async_copy(a, out.at[n], sem.at[n]) for n, a in enumerate((kept, arrived))]
        for copy in copies:
            copy.start()
        for copy in copies:
            copy.wait()


def join(kept, arrived):
    return pl.pallas_call(
        join_kernel,
        out_shape=jax.ShapeDtypeStruct((2,) + kept.shape, F32),
        in_specs=[ANY, ANY],
        out_specs=VMEM,
        scratch_shapes=[pltpu.SemaphoreType.DMA((2,))],
        compiler_params=pltpu.CompilerParams(vmem_limit_bytes=16 << 20),
        cost_estimate=SMALL,
        name="join_halves",
    )(kept, arrived)


def relay_kernel(rows, *refs):
    order = refs[0]
    sources = refs[1:-7]
    outs = refs[-6:-4]
    held, laid, sem, out_sem = refs[-4:]
    span_index = lax.axis_index("span")
    tiles = held.shape[3]

    @pl.when(place()[3])
    def _():
        for m, source in enumerate(sources):
            for t in range(tiles):
                pltpu.make_async_copy(source.at[:, :, :, tile_of(t)], held.at[m, :, :, t], sem.at[m]).start()
        for m in range(len(sources)):
            pltpu.make_async_copy(held.at[m], held.at[m], sem.at[m]).wait()
        for k in range(2):
            base = jnp.bitwise_xor(span_index, k) * rows

            def step(r, carry, k=k, base=base):
                row = order[base + r]
                away = jnp.bitwise_xor(row // rows, span_index)
                at = row % rows
                for c in range(3):
                    for t in range(tiles):
                        laid[k, c, t, pl.ds(r, 1), :] = held[away // 2, away % 2, c, t, pl.ds(at, 1), :]
                return carry

            lax.fori_loop(0, rows, step, 0, unroll=4)
            for t in range(tiles):
                pltpu.make_async_copy(laid.at[k, :, t], outs[k].at[:, :, tile_of(t)], out_sem.at[k]).start()
        for k in range(2):
            pltpu.make_async_copy(laid.at[k], laid.at[k], out_sem.at[k]).wait()


def relay(order, sources, token):
    _, _, rows, width = sources[0].shape
    piece = jax.ShapeDtypeStruct((3, rows, width), F32)
    tiles = width // LANES
    return pl.pallas_call(
        functools.partial(relay_kernel, rows),
        out_shape=[piece] * 2,
        in_specs=[SMEM] + [ANY] * (len(sources) + 1),
        out_specs=[ANY] * 2,
        scratch_shapes=[
            pltpu.VMEM((len(sources), 2, 3, tiles, rows, LANES), F32),
            pltpu.VMEM((2, 3, tiles, rows, LANES), F32),
            pltpu.SemaphoreType.DMA((len(sources),)),
            pltpu.SemaphoreType.DMA((2,)),
        ],
        compiler_params=pltpu.CompilerParams(vmem_limit_bytes=VMEM_LIMIT),
        cost_estimate=SMALL,
        name="relay_rows",
    )(order, *sources, token)


def shards(main, prec, magnet, inlet_rows):
    spans = lax.axis_size("span")
    streams = lax.axis_size("stream")
    last = streams - 1
    row_low, row_high, face_low, face_high, kept, given = pack(main, prec)
    axes = ("stream", "span")

    def hop(value, source, target, k):
        return lax.ppermute(
            value, axes, [(source * spans + a, target * spans + (a ^ k)) for a in range(spans)]
        )

    arrived = hop(given, last, last, 1)
    up_span = [(i, (i + 1) % spans) for i in range(spans)]
    up_stream = [(i, (i + 1) % streams) for i in range(streams)]
    low = lax.ppermute(row_high, "span", up_span)
    high = lax.ppermute(row_low, "span", [(b, a) for a, b in up_span])
    joined = join(kept, arrived)
    sources = [joined] + [hop(joined, last, last, 2 * m) for m in range(1, spans // 2)]
    *outs, token = interior(False, main, prec, magnet)
    face_low, face_high, token = lax.optimization_barrier((face_low, face_high, token))
    laid = relay(inlet_rows, sources, token)
    slots = [hop(laid[k], last, 0, k) for k in range(2)]
    before = lax.ppermute(face_high, "stream", up_stream)
    after = lax.ppermute(face_low, "stream", [(b, a) for a, b in up_stream])
    outs = interior(True, main, prec, magnet, (low, high, *outs))
    outs = boundary(
        ((False, True), (False, False), (True, False)),
        main, prec, magnet, low, high, before, after, (), *outs,
    )
    outs = boundary(((True, True),), main, prec, magnet, low, high, before, after, slots, *outs)
    return tuple(outs)


def solution(mesh):
    placed = P(None, "stream", "span", None)
    return jax.shard_map(
        shards,
        mesh=mesh,
        in_specs=(placed, placed, placed, P()),
        out_specs=(placed, placed),
        check_vma=False,
    )
```

profile of v0, /device:TPU:123, one launch (start us, length us, event | category | flops | bytes accessed | tf_op | source)
XLA Modules:
  0.0 74.3 jit_solution(11444974304905339657)
XLA Ops:
  0.6 4.8 %pack_halos.1 = (f32[3,28,1,1024]{3,2,1,0:T(1,128)}, f32[3,28,1,1024]{3,2,1,0:T(1,128)}, f32[3,2,32,1024]{3,2,1,0:T(8,128)}, f32[3,2,32,1024]{3,2,1,0:T(8,128)},...) custom-call(f32[3,12,32,1024]{3,2,1,0:T(8,128)} %refs_0_.11, f32[3,16,32,1024]{3,2,1,0:T(8,128)} %refs_1_.9), custom_call_target="tpu_custom_call" | custom-call | flops 1 | bytes 1 | tf_op jit(solution)/shard_map/pack_halos/pallas_call | solution.py:441
  5.4 3.8 %collective-permute-start.4 = (f32[3,32,512]{2,1,0:T(8,128)}, f32[3,32,512]{2,1,0:T(8,128)S(1)}, u32[]{:S(2)}, u32[]{:S(2)}) collective-permute-start(f32[3,32,512]{2,1,0:T(8,128)} %get-tuple-element.28), channel_id=1, source_target_pairs={{120,121},{121,120},{122,123},{123,122},{124,125},{125,124},{126,1... | collective-permute-start | bytes 589832 | tf_op jit(solution)/shard_map/ppermute | solution.py:544
  9.2 4.4 %collective-permute-done.4.arrived = f32[3,32,512]{2,1,0:T(8,128)S(1)} collective-permute-done((f32[3,32,512]{2,1,0:T(8,128)}, f32[3,32,512]{2,1,0:T(8,128)S(1)}, u32[]{:S(2)}, u32[]{:S(2)}) %collective-permute-start.4) | collective-permute-done | bytes 196640 | tf_op jit(solution)/shard_map/ppermute | solution.py:544
  13.6 0.9 %copy-done.1 = f32[3,32,512]{2,1,0:T(8,128)S(1)} copy-done((f32[3,32,512]{2,1,0:T(8,128)S(1)}, f32[3,32,512]{2,1,0:T(8,128)}, u32[]{:S(2)}) %copy-start.1) | copy-done | bytes 196632
  14.5 0.5 join_halves.1.refs_1_
  15.0 2.2 %collective-permute-start.7 = (f32[2,3,32,512]{3,2,1,0:T(8,128)S(1)}, f32[2,3,32,512]{3,2,1,0:T(8,128)S(1)}, u32[]{:S(2)}, u32[]{:S(2)}) collective-permute-start(f32[2,3,32,512]{3,2,1,0:T(8,128)S(1)} %join_halves.1.refs_1_), channel_id=1, source_target_pairs={{120,126},{121,127},{122,124},{123,125},{124,122},{125,123},{126,1... | collective-permute-start | bytes 1179656 | tf_op jit(solution)/shard_map/ppermute | solution.py:544
  17.2 9.3 %inner_rows.1 = (f32[3,12,32,1024]{3,2,1,0:T(8,128)}, f32[3,16,32,1024]{3,2,1,0:T(8,128)}, f32[8,128]{1,0:T(8,128)}) custom-call(f32[3,12,32,1024]{3,2,1,0:T(8,128)} %refs_0_.11, f32[3,16,32,1024]{3,2,1,0:T(8,128)} %refs_1_.9, f32[3,12,32,1024]{3,2,1,0:T(8,128)} %refs_2_.7), custom_call_target="tpu_custom_call" | custom-call | flops 1 | bytes 1 | tf_op jit(solution)/shard_map/inner_rows/pallas_call | solution.py:273
  26.6 0.1 collective-permute-start.2
  26.7 0.5 collective-permute-start.3
  27.2 4.1 %collective-permute-start.6 = (f32[2,3,32,512]{3,2,1,0:T(8,128)S(1)}, f32[2,3,32,512]{3,2,1,0:T(8,128)S(1)}, u32[]{:S(2)}, u32[]{:S(2)}) collective-permute-start(f32[2,3,32,512]{3,2,1,0:T(8,128)S(1)} %join_halves.1.refs_1_), channel_id=1, source_target_pairs={{120,124},{121,125},{122,126},{123,127},{124,120},{125,121},{126,1... | collective-permute-start | bytes 1179656 | tf_op jit(solution)/shard_map/ppermute | solution.py:544
  31.3 2.9 %collective-permute-start.5 = (f32[2,3,32,512]{3,2,1,0:T(8,128)S(1)}, f32[2,3,32,512]{3,2,1,0:T(8,128)S(1)}, u32[]{:S(2)}, u32[]{:S(2)}) collective-permute-start(f32[2,3,32,512]{3,2,1,0:T(8,128)S(1)} %join_halves.1.refs_1_), channel_id=1, source_target_pairs={{120,122},{121,123},{122,120},{123,121},{124,126},{125,127},{126,1... | collective-permute-start | bytes 1179656 | tf_op jit(solution)/shard_map/ppermute | solution.py:544
  34.2 0.0 collective-permute-done.7.refs_4_
  34.3 1.9 %collective-permute-start = (f32[3,28,1,1024]{3,2,1,0:T(1,128)S(1)}, f32[3,28,1,1024]{3,2,1,0:T(1,128)S(1)}, u32[]{:S(2)}, u32[]{:S(2)}) collective-permute-start(f32[3,28,1,1024]{3,2,1,0:T(1,128)S(1)} %copy-done.14), channel_id=1, source_target_pairs={{0,1},{1,2},{2,3},{3,4},{4,5},{5,6},{6,7},{7,0},{8,9},{9,10},{10,1... | collective-permute-start | bytes 1032200 | tf_op jit(solution)/shard_map/ppermute | solution.py:551
  36.2 1.1 %collective-permute-done.6.refs_3_ = f32[2,3,32,512]{3,2,1,0:T(8,128)S(1)} collective-permute-done((f32[2,3,32,512]{3,2,1,0:T(8,128)S(1)}, f32[2,3,32,512]{3,2,1,0:T(8,128)S(1)}, u32[]{:S(2)}, u32[]{:S(2)}) %collective-permute-start.6) | collective-permute-done | bytes 393248 | tf_op jit(solution)/shard_map/ppermute | solution.py:544
  37.3 2.3 %collective-permute-start.1 = (f32[3,28,1,1024]{3,2,1,0:T(1,128)S(1)}, f32[3,28,1,1024]{3,2,1,0:T(1,128)S(1)}, u32[]{:S(2)}, u32[]{:S(2)}) collective-permute-start(f32[3,28,1,1024]{3,2,1,0:T(1,128)S(1)} %copy-done.13), channel_id=1, source_target_pairs={{1,0},{2,1},{3,2},{4,3},{5,4},{6,5},{7,6},{0,7},{9,8},{10,9},{11,1... | collective-permute-start | bytes 1032200 | tf_op jit(solution)/shard_map/ppermute | solution.py:552
  39.7 8.9 %collective-permute-done.5.refs_2_ = f32[2,3,32,512]{3,2,1,0:T(8,128)S(1)} collective-permute-done((f32[2,3,32,512]{3,2,1,0:T(8,128)S(1)}, f32[2,3,32,512]{3,2,1,0:T(8,128)S(1)}, u32[]{:S(2)}, u32[]{:S(2)}) %collective-permute-start.5) | collective-permute-done | bytes 393248 | tf_op jit(solution)/shard_map/ppermute | solution.py:544
  48.6 0.8 %copy-done.8 = f32[2,3,32,512]{3,2,1,0:T(8,128)} copy-done((f32[2,3,32,512]{3,2,1,0:T(8,128)}, f32[2,3,32,512]{3,2,1,0:T(8,128)S(1)}, u32[]{:S(2)}) %copy-start.8) | copy-done | bytes 393240
  49.3 3.9 %relay_rows.1 = (f32[3,32,512]{2,1,0:T(8,128)}, f32[3,32,512]{2,1,0:T(8,128)}) custom-call(s32[256]{0:T(256)} %refs_0_.8, f32[2,3,32,512]{3,2,1,0:T(8,128)} %copy-done, f32[2,3,32,512]{3,2,1,0:T(8,128)} %copy-done.8, f32[2,3,32,512]{3,2,1,0:T(8,128)} %copy-done.7, f32[2,3,32,512]{3,2,1,0:T(8,128)} %copy-done.6, f32[8,128]{1,0:T(8,128)} %get-tuple-element.29.refs_5_), custom_call_target="tpu_custom_call" | custom-call | flops 1 | bytes 1 | tf_op jit(solution)/shard_map/relay_rows/pallas_call | solution.py:519
  53.2 1.3 %collective-permute-start.8 = (f32[3,32,512]{2,1,0:T(8,128)}, f32[3,32,512]{2,1,0:T(8,128)S(1)}, u32[]{:S(2)}, u32[]{:S(2)}) collective-permute-start(f32[3,32,512]{2,1,0:T(8,128)} %get-tuple-element.30), channel_id=1, source_target_pairs={{120,0},{121,1},{122,2},{123,3},{124,4},{125,5},{126,6},{127,7}} | collective-permute-start | bytes 589832 | tf_op jit(solution)/shard_map/ppermute | solution.py:544
  54.6 1.3 %collective-permute-start.9 = (f32[3,32,512]{2,1,0:T(8,128)}, f32[3,32,512]{2,1,0:T(8,128)S(1)}, u32[]{:S(2)}, u32[]{:S(2)}) collective-permute-start(f32[3,32,512]{2,1,0:T(8,128)} %get-tuple-element.31), channel_id=1, source_target_pairs={{120,1},{121,0},{122,3},{123,2},{124,5},{125,4},{126,7},{127,6}} | collective-permute-start | bytes 589832 | tf_op jit(solution)/shard_map/ppermute | solution.py:544
  55.9 0.0 collective-permute-done.1.refs_4_
  55.9 0.7 copy-done.5
  56.6 9.0 %edge_rows.1 = (f32[3,12,32,1024]{3,2,1,0:T(8,128)}, f32[3,16,32,1024]{3,2,1,0:T(8,128)}) custom-call(f32[3,12,32,1024]{3,2,1,0:T(8,128)} %refs_0_.11, f32[3,16,32,1024]{3,2,1,0:T(8,128)} %refs_1_.9, f32[3,12,32,1024]{3,2,1,0:T(8,128)} %refs_2_.7, f32[3,28,1,1024]{3,2,1,0:T(1,128)} %copy-done.4, ...), custom_call_target="tpu_custom_call", output_to_operand_aliasing={{0}: (5, {}), {1}: (6, {})} | custom-call | flops 1 | bytes 1 | tf_op jit(solution)/shard_map/edge_rows/pallas_call | solution.py:273
  65.6 0.0 collective-permute-done.2.refs_5_
  65.6 0.0 collective-permute-done.3.refs_6_
  65.6 0.9 %copy-done.2 = f32[3,2,32,1024]{3,2,1,0:T(8,128)} copy-done((f32[3,2,32,1024]{3,2,1,0:T(8,128)}, f32[3,2,32,1024]{3,2,1,0:T(8,128)S(1)}, u32[]{:S(2)}) %copy-start.2) | copy-done | bytes 786456
  66.5 0.3 copy-done.3
  66.8 3.9 %end_planes.1 = (f32[3,12,32,1024]{3,2,1,0:T(8,128)}, f32[3,16,32,1024]{3,2,1,0:T(8,128)}) custom-call(f32[3,12,32,1024]{3,2,1,0:T(8,128)} %refs_0_.11, f32[3,16,32,1024]{3,2,1,0:T(8,128)} %refs_1_.9, f32[3,12,32,1024]{3,2,1,0:T(8,128)} %refs_2_.7, f32[3,28,1,1024]{3,2,1,0:T(1,128)} %copy-done.4, ...), custom_call_target="tpu_custom_call", output_to_operand_aliasing={{0}: (7, {}), {1}: (8, {})} | custom-call | flops 1 | bytes 1 | tf_op jit(solution)/shard_map/end_planes/pallas_call | solution.py:375
  70.7 0.0 collective-permute-done.9.refs_8_
  70.7 0.7 copy-done.9
  71.4 0.1 copy-done.10
  71.4 2.9 %inlet_plane.1 = (f32[3,12,32,1024]{3,2,1,0:T(8,128)}, f32[3,16,32,1024]{3,2,1,0:T(8,128)}) custom-call(f32[3,12,32,1024]{3,2,1,0:T(8,128)} %refs_0_.11, f32[3,16,32,1024]{3,2,1,0:T(8,128)} %refs_1_.9, f32[3,12,32,1024]{3,2,1,0:T(8,128)} %refs_2_.7, f32[3,28,1,1024]{3,2,1,0:T(1,128)} %copy-done.4, ...), custom_call_target="tpu_custom_call", output_to_operand_aliasing={{0}: (9, {}), {1}: (10, {})} | custom-call | flops 1 | bytes 1 | tf_op jit(solution)/shard_map/inlet_plane/pallas_call | solution.py:375
  (25 shorter events, 0.1 us)
Async XLA Ops:
  5.4 8.1 %collective-permute-start.4 = (f32[3,32,512]{2,1,0:T(8,128)}, f32[3,32,512]{2,1,0:T(8,128)S(1)}, u32[]{:S(2)}, u32[]{:S(2)}) collective-permute-start(f32[3,32,512]{2,1,0:T(8,128)} %get-tuple-element.28), channel_id=1, source_target_pairs={{120,121},{121,120},{122,123},{123,122},{124,125},{125,124},{126,1... | collective-permute-start | bytes 589832 | tf_op jit(solution)/shard_map/ppermute | solution.py:544
  13.6 0.9 %copy-start.1 = (f32[3,32,512]{2,1,0:T(8,128)S(1)}, f32[3,32,512]{2,1,0:T(8,128)}, u32[]{:S(2)}) copy-start(f32[3,32,512]{2,1,0:T(8,128)} %get-tuple-element.27.kept) | copy-start | bytes 589828
  15.0 16.3 %copy-start = (f32[2,3,32,512]{3,2,1,0:T(8,128)}, f32[2,3,32,512]{3,2,1,0:T(8,128)S(1)}, u32[]{:S(2)}) copy-start(f32[2,3,32,512]{3,2,1,0:T(8,128)S(1)} %join_halves.1.refs_1_) | copy-start | bytes 1179652
  15.0 11.6 %copy-start.12 = (f32[3,2,32,1024]{3,2,1,0:T(8,128)S(1)}, f32[3,2,32,1024]{3,2,1,0:T(8,128)}, u32[]{:S(2)}) copy-start(f32[3,2,32,1024]{3,2,1,0:T(8,128)} %get-tuple-element.25) | copy-start | bytes 2359300
  15.0 11.6 %copy-start.11 = (f32[3,2,32,1024]{3,2,1,0:T(8,128)S(1)}, f32[3,2,32,1024]{3,2,1,0:T(8,128)}, u32[]{:S(2)}) copy-start(f32[3,2,32,1024]{3,2,1,0:T(8,128)} %get-tuple-element.26) | copy-start | bytes 2359300
  15.0 19.2 %copy-start.14 = (f32[3,28,1,1024]{3,2,1,0:T(1,128)S(1)}, f32[3,28,1,1024]{3,2,1,0:T(1,128)}, u32[]{:S(2)}) copy-start(f32[3,28,1,1024]{3,2,1,0:T(1,128)} %get-tuple-element.20) | copy-start | bytes 1032196
  15.0 22.3 %copy-start.13 = (f32[3,28,1,1024]{3,2,1,0:T(1,128)S(1)}, f32[3,28,1,1024]{3,2,1,0:T(1,128)}, u32[]{:S(2)}) copy-start(f32[3,28,1,1024]{3,2,1,0:T(1,128)} %get-tuple-element.21) | copy-start | bytes 1032196
  15.0 19.2 %collective-permute-start.7 = (f32[2,3,32,512]{3,2,1,0:T(8,128)S(1)}, f32[2,3,32,512]{3,2,1,0:T(8,128)S(1)}, u32[]{:S(2)}, u32[]{:S(2)}) collective-permute-start(f32[2,3,32,512]{3,2,1,0:T(8,128)S(1)} %join_halves.1.refs_1_), channel_id=1, source_target_pairs={{120,126},{121,127},{122,124},{123,125},{124,122},{125,123},{126,1... | collective-permute-start | bytes 1179656 | tf_op jit(solution)/shard_map/ppermute | solution.py:544
  26.6 39.0 %collective-permute-start.2 = (f32[3,2,32,1024]{3,2,1,0:T(8,128)S(1)}, f32[3,2,32,1024]{3,2,1,0:T(8,128)S(1)}, u32[]{:S(2)}, u32[]{:S(2)}) collective-permute-start(f32[3,2,32,1024]{3,2,1,0:T(8,128)S(1)} %copy-done.12), channel_id=1, source_target_pairs={{0,8},{8,16},{16,24},{24,32},{32,40},{40,48},{48,56},{56,64},{64,7... | collective-permute-start | bytes 2359304 | tf_op jit(solution)/shard_map/ppermute | solution.py:559
  26.7 38.9 %collective-permute-start.3 = (f32[3,2,32,1024]{3,2,1,0:T(8,128)S(1)}, f32[3,2,32,1024]{3,2,1,0:T(8,128)S(1)}, u32[]{:S(2)}, u32[]{:S(2)}) collective-permute-start(f32[3,2,32,1024]{3,2,1,0:T(8,128)S(1)} %copy-done.11), channel_id=1, source_target_pairs={{8,0},{16,8},{24,16},{32,24},{40,32},{48,40},{56,48},{64,56},{72,6... | collective-permute-start | bytes 2359304 | tf_op jit(solution)/shard_map/ppermute | solution.py:560
  27.2 10.2 %collective-permute-start.6 = (f32[2,3,32,512]{3,2,1,0:T(8,128)S(1)}, f32[2,3,32,512]{3,2,1,0:T(8,128)S(1)}, u32[]{:S(2)}, u32[]{:S(2)}) collective-permute-start(f32[2,3,32,512]{3,2,1,0:T(8,128)S(1)} %join_halves.1.refs_1_), channel_id=1, source_target_pairs={{120,124},{121,125},{122,126},{123,127},{124,120},{125,121},{126,1... | collective-permute-start | bytes 1179656 | tf_op jit(solution)/shard_map/ppermute | solution.py:544
  31.3 17.2 %collective-permute-start.5 = (f32[2,3,32,512]{3,2,1,0:T(8,128)S(1)}, f32[2,3,32,512]{3,2,1,0:T(8,128)S(1)}, u32[]{:S(2)}, u32[]{:S(2)}) collective-permute-start(f32[2,3,32,512]{3,2,1,0:T(8,128)S(1)} %join_halves.1.refs_1_), channel_id=1, source_target_pairs={{120,122},{121,123},{122,120},{123,121},{124,126},{125,127},{126,1... | collective-permute-start | bytes 1179656 | tf_op jit(solution)/shard_map/ppermute | solution.py:544
  34.2 14.3 %copy-start.6 = (f32[2,3,32,512]{3,2,1,0:T(8,128)}, f32[2,3,32,512]{3,2,1,0:T(8,128)S(1)}, u32[]{:S(2)}) copy-start(f32[2,3,32,512]{3,2,1,0:T(8,128)S(1)} %collective-permute-done.7.refs_4_) | copy-start | bytes 1179652
  34.3 20.3 %collective-permute-start = (f32[3,28,1,1024]{3,2,1,0:T(1,128)S(1)}, f32[3,28,1,1024]{3,2,1,0:T(1,128)S(1)}, u32[]{:S(2)}, u32[]{:S(2)}) collective-permute-start(f32[3,28,1,1024]{3,2,1,0:T(1,128)S(1)} %copy-done.14), channel_id=1, source_target_pairs={{0,1},{1,2},{2,3},{3,4},{4,5},{5,6},{6,7},{7,0},{8,9},{9,10},{10,1... | collective-permute-start | bytes 1032200 | tf_op jit(solution)/shard_map/ppermute | solution.py:551
  37.3 11.2 %copy-start.7 = (f32[2,3,32,512]{3,2,1,0:T(8,128)}, f32[2,3,32,512]{3,2,1,0:T(8,128)S(1)}, u32[]{:S(2)}) copy-start(f32[2,3,32,512]{3,2,1,0:T(8,128)S(1)} %collective-permute-done.6.refs_3_) | copy-start | bytes 1179652
  37.3 18.6 %collective-permute-start.1 = (f32[3,28,1,1024]{3,2,1,0:T(1,128)S(1)}, f32[3,28,1,1024]{3,2,1,0:T(1,128)S(1)}, u32[]{:S(2)}, u32[]{:S(2)}) collective-permute-start(f32[3,28,1,1024]{3,2,1,0:T(1,128)S(1)} %copy-done.13), channel_id=1, source_target_pairs={{1,0},{2,1},{3,2},{4,3},{5,4},{6,5},{7,6},{0,7},{9,8},{10,9},{11,1... | collective-permute-start | bytes 1032200 | tf_op jit(solution)/shard_map/ppermute | solution.py:552
  48.6 0.8 %copy-start.8 = (f32[2,3,32,512]{3,2,1,0:T(8,128)}, f32[2,3,32,512]{3,2,1,0:T(8,128)S(1)}, u32[]{:S(2)}) copy-start(f32[2,3,32,512]{3,2,1,0:T(8,128)S(1)} %collective-permute-done.5.refs_2_) | copy-start | bytes 1179652
  53.2 17.4 %collective-permute-start.8 = (f32[3,32,512]{2,1,0:T(8,128)}, f32[3,32,512]{2,1,0:T(8,128)S(1)}, u32[]{:S(2)}, u32[]{:S(2)}) collective-permute-start(f32[3,32,512]{2,1,0:T(8,128)} %get-tuple-element.30), channel_id=1, source_target_pairs={{120,0},{121,1},{122,2},{123,3},{124,4},{125,5},{126,6},{127,7}} | collective-permute-start | bytes 589832 | tf_op jit(solution)/shard_map/ppermute | solution.py:544
  54.6 1.3 %copy-start.4 = (f32[3,28,1,1024]{3,2,1,0:T(1,128)}, f32[3,28,1,1024]{3,2,1,0:T(1,128)S(1)}, u32[]{:S(2)}) copy-start(f32[3,28,1,1024]{3,2,1,0:T(1,128)S(1)} %collective-permute-done.refs_3_) | copy-start | bytes 1032196
  54.6 16.1 %collective-permute-start.9 = (f32[3,32,512]{2,1,0:T(8,128)}, f32[3,32,512]{2,1,0:T(8,128)S(1)}, u32[]{:S(2)}, u32[]{:S(2)}) collective-permute-start(f32[3,32,512]{2,1,0:T(8,128)} %get-tuple-element.31), channel_id=1, source_target_pairs={{120,1},{121,0},{122,3},{123,2},{124,5},{125,4},{126,7},{127,6}} | collective-permute-start | bytes 589832 | tf_op jit(solution)/shard_map/ppermute | solution.py:544
  55.9 0.7 copy-start.5
  65.6 0.9 %copy-start.2 = (f32[3,2,32,1024]{3,2,1,0:T(8,128)}, f32[3,2,32,1024]{3,2,1,0:T(8,128)S(1)}, u32[]{:S(2)}) copy-start(f32[3,2,32,1024]{3,2,1,0:T(8,128)S(1)} %collective-permute-done.2.refs_5_) | copy-start | bytes 2359300
  65.6 1.2 %copy-start.3 = (f32[3,2,32,1024]{3,2,1,0:T(8,128)}, f32[3,2,32,1024]{3,2,1,0:T(8,128)S(1)}, u32[]{:S(2)}) copy-start(f32[3,2,32,1024]{3,2,1,0:T(8,128)S(1)} %collective-permute-done.3.refs_6_) | copy-start | bytes 2359300
  70.7 0.7 copy-start.9
  70.7 0.7 copy-start.10
where the time goes:
time: 74.7 us; the launch traced here: 74.3 us
  Pallas kernels  34.2 us (46%)
  starting transfers between devices  20.4 us (27%)
  waiting for transfers between devices  14.4 us (19%)
  local copies, waits for them, and re-layouts  4.31 us (6%)
  between operations  0.93 us (1%)
    pallas_call x2, Pallas kernels, interior(): pl.pallas_call(functools.partial(interior_kernel, edges, n_main, n_prec,...  18.3 us
    ppermute x6, starting transfers between devices, hop(): lax.ppermute(value, axes, [(source * spans + a, target * spans + (a ^ k))...  15.6 us
    ppermute x6, waiting for transfers between devices, hop(): lax.ppermute(value, axes, [(source * spans + a, target * spans + (a ^ k))...  14.4 us
    pallas_call x2, Pallas kernels, boundary(): pl.pallas_call(functools.partial(boundary_kernel, n_main, n_prec, rows, j...  6.72 us
    pallas_call x1, Pallas kernels, pack(): pl.pallas_call(functools.partial(pack_kernel, n_main, n_prec, rows, depth...  4.8 us
    unnamed x30, local copies, waits for them, and re-layouts  4.31 us
    pallas_call x1, Pallas kernels, relay(): pl.pallas_call(functools.partial(relay_kernel, rows), out_shape=[piece] *...  3.91 us
    ppermute x1, starting transfers between devices, shards(): high = lax.ppermute(row_low, 'span', [(b, a) for a, b in up_span])  2.34 us
  transfers between devices with their start and end apart: 10, of which 3 were waited for; matrix products, arithmetic and copies ran while one was open for 0% of the time, Pallas kernels for 35%

commit v1 on v0

v1 whole, which is shorter than its diff:
```python
import functools

import jax
import jax.numpy as jnp
from jax import lax
from jax.experimental import pallas as pl
from jax.experimental.pallas import tpu as pltpu
from jax.sharding import PartitionSpec as P

TIME_STEP = 0.1
VISCOSITY = 0.02
SMAGORINSKY = 0.03
INTERACTION = 0.5

LANES = 128
SUBLANES = 8


def cost(micros):
    return pl.CostEstimate(flops=0, bytes_accessed=int(micros * 3.7e6), transcendentals=0)


def in_hbm(value):
    return pltpu.with_memory_space_constraint(value, pltpu.HBM)


F32 = jnp.float32
ANY = pl.BlockSpec(memory_space=pl.ANY)
HBM = pl.BlockSpec(memory_space=pltpu.HBM)
VMEM = pl.BlockSpec(memory_space=pltpu.VMEM)
SMEM = pl.BlockSpec(memory_space=pltpu.SMEM)

EDDY_SCALE = (TIME_STEP * SMAGORINSKY) ** 2 / 4.0
EDDY_FLOOR = (TIME_STEP * SMAGORINSKY) ** 2 * 1e-06


def update(u, forward, backward, magnet):
    diff = [[forward[j][i] - backward[j][i] for j in range(3)] for i in range(3)]
    diag = diff[0][0] * diff[0][0] + diff[1][1] * diff[1][1] + diff[2][2] * diff[2][2]
    quad = diag + diag
    for i, j in ((0, 1), (0, 2), (1, 2)):
        pair = diff[i][j] + diff[j][i]
        quad = quad + pair * pair
    square = quad * EDDY_SCALE + EDDY_FLOOR
    eddy = square * lax.rsqrt(square)
    visc = eddy + TIME_STEP * VISCOSITY
    keep = (1.0 - 6.0 * TIME_STEP * VISCOSITY) - 6.0 * eddy
    if magnet is not None:
        scale = TIME_STEP * INTERACTION
        aligned = (u[0] * magnet[0] + u[1] * magnet[1] + u[2] * magnet[2]) * scale
        strength = magnet[0] * magnet[0] + magnet[1] * magnet[1] + magnet[2] * magnet[2]
        keep = keep - strength * scale
    speed = [u[j] * (-0.5 * TIME_STEP) for j in range(3)]
    out = []
    for i in range(3):
        around = (forward[0][i] + backward[0][i]) + (forward[1][i] + backward[1][i])
        around = around + (forward[2][i] + backward[2][i])
        value = keep * u[i] + visc * around
        value = value + speed[0] * diff[i][0] + speed[1] * diff[i][1] + speed[2] * diff[i][2]
        if magnet is not None:
            value = value + aligned * magnet[i]
        out.append(value)
    return out


def shifted_lanes(read, tiles):
    shape = (SUBLANES, LANES)
    lane = lax.broadcasted_iota(jnp.int32, shape, 1)
    zero = jnp.zeros(shape, F32)
    here = read(0)
    left = zero
    ahead = pltpu.roll(here, LANES - 1, 1)
    for t in range(tiles):
        behind = pltpu.roll(here, 1, 1)
        following = read(t + 1) if t + 1 < tiles else None
        right = pltpu.roll(following, LANES - 1, 1) if t + 1 < tiles else zero
        yield here, jnp.where(lane == LANES - 1, right, ahead), jnp.where(lane == 0, left, behind)
        here, left, ahead = following, behind, right


def plane_rows(center, low, high, before, after, magnet, store, tiles):
    streams = [shifted_lanes(lambda t, c=c: center(c, t), tiles) for c in range(3)]
    for t in range(tiles):
        along = [next(stream) for stream in streams]
        u = [value[0] for value in along]
        forward = [
            [after(c, t) for c in range(3)],
            [high(c, t) for c in range(3)],
            [value[1] for value in along],
        ]
        backward = [
            [before(c, t) for c in range(3)],
            [low(c, t) for c in range(3)],
            [value[2] for value in along],
        ]
        field = None if magnet is None else [magnet(c, t) for c in range(3)]
        for c, value in enumerate(update(u, forward, backward, field)):
            store(c, t, value)


BASE = SUBLANES
GROUP = 4


def tile_of(t):
    return pl.ds(t * LANES, LANES)


def rows_of(ref, x, at):
    return lambda c, t: ref[c, x, t, pl.ds(at, SUBLANES), :]


def span_of(ref, x, at):
    return lambda c, t: ref[c, x, pl.ds(at, SUBLANES), tile_of(t)]


def span_rows(ref, c, t, k):
    return ref[c, pl.ds(k * SUBLANES, SUBLANES), tile_of(t)]


def with_row(inside, halo, x, edge):
    def read(c, t):
        sub = lax.broadcasted_iota(jnp.int32, (SUBLANES, LANES), 0)
        row = jnp.broadcast_to(halo[c, x, :, tile_of(t)], (SUBLANES, LANES))
        return jnp.where(sub == edge, row, inside(c, t))

    return read


def edge_of(flow, low, high, x, k, last):
    at = BASE + k * SUBLANES
    below, above = rows_of(flow, x, at - 1), rows_of(flow, x, at + 1)
    if k == 0:
        below = with_row(below, low, x, 0)
    if k == last:
        above = with_row(above, high, x, SUBLANES - 1)
    return below, above


def place():
    span, stream = lax.axis_index("span"), lax.axis_index("stream")
    return span == 0, span == lax.axis_size("span") - 1, stream == 0, stream == lax.axis_size("stream") - 1


def wait_part(part, sem):
    pltpu.make_async_copy(part, part, sem).wait()


def interior_kernel(edges, n_main, n_prec, rows, *refs):
    if edges:
        flow, magnet, low, high, _, _, main_out, prec_out, field, result, field_sem, out_sem = refs
    else:
        main, prec, magnet, main_out, prec_out, flow, face_low, face_high = refs[:8]
        field, result, field_sem, out_sem, in_sem, face_sem = refs[8:]
    tiles = flow.shape[2]
    total = n_main + n_prec
    last = rows // SUBLANES - 1
    kept = [0, last] if edges else list(range(1, last))
    if edges:
        spans = [(0, 0, SUBLANES), (SUBLANES, last * SUBLANES, SUBLANES)]
    else:
        spans = [(0, SUBLANES, (last - 1) * SUBLANES)]

    def load(source, x, i):
        for t in range(tiles):
            pltpu.make_async_copy(
                source.at[:, pl.ds(x, GROUP), :, tile_of(t)],
                flow.at[:, pl.ds(i, GROUP), t, pl.ds(BASE, rows)],
                in_sem.at[i // GROUP],
            ).start()

    def load_field(x):
        for at, row, size in spans:
            pltpu.make_async_copy(
                magnet.at[:, pl.ds(x, GROUP), pl.ds(row, size)],
                field.at[:, pl.ds(x, GROUP), pl.ds(at, size)],
                field_sem.at[x // GROUP],
            ).start()

    def wait_flow(g):
        if not edges:
            wait_part(flow.at[:, pl.ds(0, GROUP), :, pl.ds(BASE, rows)], in_sem.at[g])

    def wait_field(g):
        wait_part(field.at[:, pl.ds(0, GROUP)], field_sem.at[g])

    if not edges:
        for x in range(0, n_prec, GROUP):
            load(prec, x, x)
    for x in range(0, n_main, GROUP):
        if not edges:
            load(main, x, n_prec + x)
        load_field(x)
    faces = []
    if not edges:
        for kind, source, count in ((0, main, n_main), (1, prec, n_prec)):
            faces.append((source.at[:, 0], face_low.at[:, kind]))
            faces.append((source.at[:, count - 1], face_high.at[:, kind]))
        faces = [pltpu.make_async_copy(a, b, face_sem.at[n]) for n, (a, b) in enumerate(faces)]
        for copy in faces:
            copy.start()

    def run(target, x, i, with_field):
        for n, k in enumerate(kept):
            at = BASE + k * SUBLANES

            def store(c, t, value, n=n):
                result[c, i, pl.ds(n * SUBLANES, SUBLANES), tile_of(t)] = value

            if edges:
                below, above = edge_of(flow, low, high, i, k, last)
            else:
                below, above = rows_of(flow, i, at - 1), rows_of(flow, i, at + 1)
            plane_rows(
                rows_of(flow, i, at),
                below,
                above,
                rows_of(flow, i - 1, at),
                rows_of(flow, i + 1, at),
                span_of(field, x, n * SUBLANES) if with_field else None,
                store,
                tiles,
            )
        for at, row, size in spans:
            pltpu.make_async_copy(
                result.at[:, i, pl.ds(at, size)], target.at[:, x, pl.ds(row, size)], out_sem.at[i]
            ).start()

    wait_flow(0)

    def prec_step(x, carry):
        @pl.when((x + 1) % GROUP == 0)
        def _():
            wait_flow((x + 1) // GROUP)

        run(prec_out, x, x, False)
        return carry

    lax.fori_loop(1, n_prec - 1, prec_step, 0)
    wait_flow(n_prec // GROUP)
    wait_field(0)

    def main_step(x, carry):
        @pl.when((x + 1) % GROUP == 0)
        def _():
            wait_flow((n_prec + x + 1) // GROUP)
            wait_field((x + 1) // GROUP)

        run(main_out, x, n_prec + x, True)
        return carry

    lax.fori_loop(1, n_main - 1, main_step, 0)
    for copy in faces:
        copy.wait()

    def drain(i, carry):
        wait_part(result.at[:, 0], out_sem.at[i])
        return carry

    lax.fori_loop(1, n_prec - 1, drain, 0)
    lax.fori_loop(n_prec + 1, total - 1, drain, 0)


def interior(edges, main_shape, prec_shape, operands):
    _, n_main, rows, depth = main_shape
    n_prec = prec_shape[1]
    total = n_main + n_prec
    kept = 2 * SUBLANES if edges else rows - 2 * SUBLANES
    scratch = [
        pltpu.VMEM((3, n_main, kept, depth), F32),
        pltpu.VMEM((3, total, kept, depth), F32),
        pltpu.SemaphoreType.DMA((n_main // GROUP,)),
        pltpu.SemaphoreType.DMA((total,)),
    ]
    outs = [jax.ShapeDtypeStruct(main_shape, F32), jax.ShapeDtypeStruct(prec_shape, F32)]
    out_specs = [HBM, HBM]
    if edges:
        specs = [VMEM, HBM, VMEM, VMEM, HBM, HBM]
        aliases = {4: 0, 5: 1}
    else:
        specs = [HBM] * 3
        aliases = {}
        scratch += [pltpu.SemaphoreType.DMA((total // GROUP,)), pltpu.SemaphoreType.DMA((4,))]
        outs.append(pltpu.VMEM((3, total, depth // LANES, rows + 2 * SUBLANES, LANES), F32))
        outs += [pltpu.VMEM((3, 2, rows, depth), F32)] * 2
        out_specs += [VMEM] * 3
    return pl.pallas_call(
        functools.partial(interior_kernel, edges, n_main, n_prec, rows),
        out_shape=outs,
        in_specs=specs,
        out_specs=out_specs,
        scratch_shapes=scratch,
        input_output_aliases=aliases,
        compiler_params=pltpu.CompilerParams(vmem_limit_bytes=16 << 20),
        cost_estimate=cost(8 if edges else 9),
        name="edge_rows" if edges else "inner_rows",
    )(*operands)


def boundary_kernel(n_main, n_prec, rows, jobs, chunks, *refs):
    flow, magnet, low, high, before, after = refs[:6]
    slots = refs[6 : 6 + chunks]
    main_out, prec_out, field, result, field_sem, out_sem = refs[8 + chunks :]
    last = rows // SUBLANES - 1
    tiles = flow.shape[2]
    _, _, at_inlet, at_outlet = place()
    for job, (is_main, at_low) in enumerate(jobs):
        if is_main:
            x = 0 if at_low else n_main - 1
            pltpu.make_async_copy(magnet.at[:, x], field.at[:, job], field_sem.at[job]).start()
    for job, (is_main, at_low) in enumerate(jobs):
        x = 0 if at_low else (n_main if is_main else n_prec) - 1
        i = n_prec + x if is_main else x
        if is_main:
            wait_part(field.at[:, job], field_sem.at[job])
        for k in range(last + 1):
            at = BASE + k * SUBLANES
            center = rows_of(flow, i, at)
            face = span_of(before if at_low else after, 0 if is_main else 1, k * SUBLANES)

            def store(c, t, value, job=job, k=k):
                result[c, job, pl.ds(k * SUBLANES, SUBLANES), tile_of(t)] = value

            def inlet(c, t, k=k, face=face):
                fed = span_rows(slots[0], c, t, k) + span_rows(slots[1], c, t, k)
                return jnp.where(at_inlet, fed, face(c, t))

            def outlet(c, t, center=center, face=face):
                return jnp.where(at_outlet, center(c, t), face(c, t))

            if is_main:
                face_side = inlet if at_low else outlet
            else:
                face_side = face
            below, above = edge_of(flow, low, high, i, k, last)
            plane_rows(
                center,
                below,
                above,
                face_side if at_low else rows_of(flow, i - 1, at),
                rows_of(flow, i + 1, at) if at_low else face_side,
                span_of(field, job, k * SUBLANES) if is_main else None,
                store,
                tiles,
            )
        target = main_out if is_main else prec_out
        pltpu.make_async_copy(result.at[:, job], target.at[:, x], out_sem.at[job]).start()
    for job in range(len(jobs)):
        wait_part(result.at[:, job], out_sem.at[job])


def boundary(jobs, n_main, n_prec, flow, magnet, low, high, before, after, slots, main_out, prec_out):
    _, _, rows, depth = magnet.shape
    count = len(jobs)
    chunks = len(slots)
    return pl.pallas_call(
        functools.partial(boundary_kernel, n_main, n_prec, rows, jobs, chunks),
        out_shape=[jax.ShapeDtypeStruct(main_out.shape, F32), jax.ShapeDtypeStruct(prec_out.shape, F32)],
        in_specs=[VMEM, HBM] + [VMEM] * (4 + chunks) + [HBM] * 2,
        out_specs=[HBM, HBM],
        scratch_shapes=[
            pltpu.VMEM((3, count, rows, depth), F32),
            pltpu.VMEM((3, count, rows, depth), F32),
            pltpu.SemaphoreType.DMA((count,)),
            pltpu.SemaphoreType.DMA((count,)),
        ],
        input_output_aliases={6 + chunks: 0, 7 + chunks: 1},
        compiler_params=pltpu.CompilerParams(vmem_limit_bytes=8 << 20),
        cost_estimate=cost(len(jobs)),
        name="end_planes",
    )(flow, magnet, low, high, before, after, *slots, main_out, prec_out)


def outlet_kernel(prec, plane, sem):
    copy = pltpu.make_async_copy(prec.at[:, prec.shape[1] - 1], plane, sem)
    copy.start()
    copy.wait()


def outlet(prec):
    _, _, rows, depth = prec.shape
    return pl.pallas_call(
        outlet_kernel,
        out_shape=pltpu.VMEM((3, rows, depth), F32),
        in_specs=[HBM],
        out_specs=VMEM,
        scratch_shapes=[pltpu.SemaphoreType.DMA],
        compiler_params=pltpu.CompilerParams(vmem_limit_bytes=2 << 20),
        cost_estimate=cost(1),
        name="outlet_plane",
    )(prec)


def pack_kernel(n_main, n_prec, rows, *refs):
    main, prec, row_low, row_high, low_tile, high_tile, sem = refs
    first, last = pl.ds(0, SUBLANES), pl.ds(rows - SUBLANES, SUBLANES)
    groups = [(prec, g, g) for g in range(0, n_prec, GROUP)] + [(main, g, n_prec + g) for g in range(0, n_main, GROUP)]
    copies = []
    for n, (source, x, i) in enumerate(groups):
        for m, (part, target) in enumerate(((first, low_tile), (last, high_tile))):
            copies.append(
                pltpu.make_async_copy(
                    source.at[:, pl.ds(x, GROUP), part], target.at[:, pl.ds(i, GROUP)], sem.at[2 * n + m]
                )
            )
    for copy in copies:
        copy.start()
    low_wall, high_wall, _, _ = place()
    for n, (_, _, i) in enumerate(groups):
        copies[2 * n].wait()
        copies[2 * n + 1].wait()
        for c in range(3):
            for x in range(i, i + GROUP):
                row_low[c, x] = low_tile[c, x, pl.ds(0, 1), :]
                row_high[c, x] = high_tile[c, x, pl.ds(SUBLANES - 1, 1), :]

    @pl.when(low_wall)
    def _():
        row_low[...] = jnp.zeros_like(row_low)

    @pl.when(high_wall)
    def _():
        row_high[...] = jnp.zeros_like(row_high)


def pack(main, prec):
    _, n_main, rows, depth = main.shape
    n_prec = prec.shape[1]
    total = n_main + n_prec
    packed = pltpu.VMEM((3, total, 1, depth), F32)
    return pl.pallas_call(
        functools.partial(pack_kernel, n_main, n_prec, rows),
        out_shape=[packed, packed],
        in_specs=[HBM, HBM],
        out_specs=[VMEM] * 2,
        scratch_shapes=[
            pltpu.VMEM((3, total, SUBLANES, depth), F32),
            pltpu.VMEM((3, total, SUBLANES, depth), F32),
            pltpu.SemaphoreType.DMA((2 * total // GROUP,)),
        ],
        compiler_params=pltpu.CompilerParams(vmem_limit_bytes=12 << 20),
        cost_estimate=cost(3),
        name="pack_rows",
    )(main, prec)


def relay_kernel(rows, *refs):
    order = refs[0]
    sources = refs[1:-6]
    outs = refs[-6:-4]
    held, laid, sem, out_sem = refs[-4:]
    span_index = lax.axis_index("span")
    tiles = held.shape[2]

    @pl.when(lax.axis_index("stream") == lax.axis_size("stream") - 2)
    def _():
        for m, source in enumerate(sources):
            for t in range(tiles):
                pltpu.make_async_copy(source.at[:, :, tile_of(t)], held.at[m, :, t], sem.at[m]).start()
        laid[...] = jnp.zeros_like(laid)
        for m in range(len(sources)):
            wait_part(held.at[m], sem.at[m])
        for k in range(2):
            base = jnp.bitwise_xor(span_index, k) * rows

            def step(r, carry, k=k, base=base):
                row = order[base + r]
                away = jnp.bitwise_xor(row // rows, span_index)
                at = row % rows

                @pl.when(away % 2 == 0)
                def _():
                    for c in range(3):
                        for t in range(tiles):
                            laid[k, c, t, pl.ds(r, 1), :] = held[away // 2, c, t, pl.ds(at, 1), :]

                return carry

            lax.fori_loop(0, rows, step, 0)
            for t in range(tiles):
                pltpu.make_async_copy(laid.at[k, :, t], outs[k].at[:, :, tile_of(t)], out_sem.at[k]).start()
        for k in range(2):
            wait_part(laid.at[k], out_sem.at[k])


def relay(order, sources):
    _, rows, depth = sources[0].shape
    piece = pltpu.VMEM((3, rows, depth), F32)
    tiles = depth // LANES
    return pl.pallas_call(
        functools.partial(relay_kernel, rows),
        out_shape=[piece] * 2,
        in_specs=[SMEM] + [VMEM] * len(sources),
        out_specs=[VMEM] * 2,
        scratch_shapes=[
            pltpu.VMEM((len(sources), 3, tiles, rows, LANES), F32),
            pltpu.VMEM((2, 3, tiles, rows, LANES), F32),
            pltpu.SemaphoreType.DMA((len(sources),)),
            pltpu.SemaphoreType.DMA((2,)),
        ],
        compiler_params=pltpu.CompilerParams(vmem_limit_bytes=8 << 20),
        cost_estimate=cost(1),
        name="relay_rows",
    )(order, *sources)


def shards(main, prec, magnet, inlet_rows):
    spans = lax.axis_size("span")
    streams = lax.axis_size("stream")
    last = streams - 1
    n_main, n_prec = main.shape[1], prec.shape[1]
    main, prec, magnet = in_hbm(main), in_hbm(prec), in_hbm(magnet)
    axes = ("stream", "span")

    def hop(value, source, target, k):
        return lax.ppermute(
            value, axes, [(source * spans + a, target * spans + (a ^ k)) for a in range(spans)]
        )

    plane = outlet(prec)
    sources = [hop(plane, last, last - 1, 2 * m) for m in range(spans // 2)]
    row_low, row_high = pack(main, prec)
    row_low, row_high, sources[0] = lax.optimization_barrier((row_low, row_high, sources[0]))
    up_span = [(i, (i + 1) % spans) for i in range(spans)]
    up_stream = [(i, (i + 1) % streams) for i in range(streams)]
    low = lax.ppermute(row_high, "span", up_span)
    high = lax.ppermute(row_low, "span", [(b, a) for a, b in up_span])
    *outs, flow, face_low, face_high = interior(False, main.shape, prec.shape, (main, prec, magnet))
    face_low, face_high, low, high, *sources = lax.optimization_barrier((face_low, face_high, low, high, *sources))
    before = lax.ppermute(face_high, "stream", up_stream)
    after = lax.ppermute(face_low, "stream", [(b, a) for a, b in up_stream])
    laid = relay(inlet_rows, sources)
    slots = [hop(laid[k], last - 1, 0, k) for k in range(2)]
    outs = interior(True, main.shape, prec.shape, (flow, magnet, low, high, *outs))
    ends = ((False, True), (False, False), (True, False), (True, True))
    outs = boundary(ends, n_main, n_prec, flow, magnet, low, high, before, after, slots, *outs)
    return tuple(outs)


def solution(mesh):
    placed = P(None, "stream", "span", None)
    return jax.shard_map(
        shards,
        mesh=mesh,
        in_specs=(placed, placed, placed, P()),
        out_specs=(placed, placed),
        check_vma=False,
    )
```

time: 74.7 us -> 56.2 us (0.75)
  the two profiles are of different devices: /device:TPU:123 before, /device:TPU:0 now
where the time goes in v1:
time: 56.2 us; the launch traced here: 56 us
  Pallas kernels  23.6 us (42%)
  starting transfers between devices  19 us (34%)
  waiting for transfers between devices  12.6 us (22%)
  between operations  0.77 us (1%)
    pallas_call x2, Pallas kernels, interior(): pl.pallas_call(functools.partial(interior_kernel, edges, n_main, n_prec,...  16.3 us
    ppermute x1, starting transfers between devices, shards(): after = lax.ppermute(face_low, 'stream', [(b, a) for a, b in up_stream])  8 us
    ppermute x6, waiting for transfers between devices, hop(): lax.ppermute(value, axes, [(source * spans + a, target * spans + (a ^ k))...  7.44 us
    ppermute x6, starting transfers between devices, hop(): lax.ppermute(value, axes, [(source * spans + a, target * spans + (a ^ k))...  5.33 us
    ppermute x1, waiting for transfers between devices, shards(): high = lax.ppermute(row_low, 'span', [(b, a) for a, b in up_span])  5.17 us
    ppermute x1, starting transfers between devices, shards(): low = lax.ppermute(row_high, 'span', up_span)  3.16 us
    pallas_call x1, Pallas kernels, boundary(): pl.pallas_call(functools.partial(boundary_kernel, n_main, n_prec, rows, j...  2.89 us
    pallas_call x1, Pallas kernels, pack(): pl.pallas_call(functools.partial(pack_kernel, n_main, n_prec, rows), out_...  2.72 us
  transfers between devices with their start and end apart: 10, of which 2 were waited for; matrix products, arithmetic and copies ran while one was open for 0% of the time, Pallas kernels for 35%

profile of v1, /device:TPU:0, one launch (start us, length us, event | category | flops | bytes accessed | tf_op | source)
XLA Modules:
  0.0 56.0 jit_solution(14325006796671850126)
XLA Ops:
  0.6 1.0 %outlet_plane.1 = f32[3,32,1024]{2,1,0:T(8,128)S(1)} custom-call(f32[3,16,32,1024]{3,2,1,0:T(8,128)} %prec.1), custom_call_target="tpu_custom_call" | custom-call | bytes 3700000 | tf_op jit(solution)/shard_map/outlet_plane/pallas_call | solution.py:382
  1.6 0.7 %collective-permute-start = (f32[3,32,1024]{2,1,0:T(8,128)S(1)}, f32[3,32,1024]{2,1,0:T(8,128)S(1)}, u32[]{:S(2)}, u32[]{:S(2)}) collective-permute-start(f32[3,32,1024]{2,1,0:T(8,128)S(1)} %outlet_plane.1), channel_id=1, source_target_pairs={{120,112},{121,113},{122,114},{123,115},{124,116},{125,117},{126,1... | collective-permute-start | bytes 1179656 | tf_op jit(solution)/shard_map/ppermute | solution.py:516
  2.3 0.7 %collective-permute-start.3 = (f32[3,32,1024]{2,1,0:T(8,128)S(1)}, f32[3,32,1024]{2,1,0:T(8,128)S(1)}, u32[]{:S(2)}, u32[]{:S(2)}) collective-permute-start(f32[3,32,1024]{2,1,0:T(8,128)S(1)} %outlet_plane.1), channel_id=1, source_target_pairs={{120,114},{121,115},{122,112},{123,113},{124,118},{125,119},{126,1... | collective-permute-start | bytes 1179656 | tf_op jit(solution)/shard_map/ppermute | solution.py:516
  3.0 0.7 %collective-permute-start.4 = (f32[3,32,1024]{2,1,0:T(8,128)S(1)}, f32[3,32,1024]{2,1,0:T(8,128)S(1)}, u32[]{:S(2)}, u32[]{:S(2)}) collective-permute-start(f32[3,32,1024]{2,1,0:T(8,128)S(1)} %outlet_plane.1), channel_id=1, source_target_pairs={{120,116},{121,117},{122,118},{123,119},{124,112},{125,113},{126,1... | collective-permute-start | bytes 1179656 | tf_op jit(solution)/shard_map/ppermute | solution.py:516
  3.7 0.7 %collective-permute-start.5 = (f32[3,32,1024]{2,1,0:T(8,128)S(1)}, f32[3,32,1024]{2,1,0:T(8,128)S(1)}, u32[]{:S(2)}, u32[]{:S(2)}) collective-permute-start(f32[3,32,1024]{2,1,0:T(8,128)S(1)} %outlet_plane.1), channel_id=1, source_target_pairs={{120,118},{121,119},{122,116},{123,117},{124,114},{125,115},{126,1... | collective-permute-start | bytes 1179656 | tf_op jit(solution)/shard_map/ppermute | solution.py:516
  4.4 2.7 %pack_rows.1 = (f32[3,28,1,1024]{3,2,1,0:T(1,128)S(1)}, f32[3,28,1,1024]{3,2,1,0:T(1,128)S(1)}) custom-call(f32[3,12,32,1024]{3,2,1,0:T(8,128)} %refs_0_.4, f32[3,16,32,1024]{3,2,1,0:T(8,128)} %prec.1), custom_call_target="tpu_custom_call" | custom-call | bytes 11100000 | tf_op jit(solution)/shard_map/pack_rows/pallas_call | solution.py:431
  7.2 0.0 collective-permute-done.refs_1_
  7.2 0.0 copy-start
  7.2 3.2 %collective-permute-start.1 = (f32[3,28,1,1024]{3,2,1,0:T(1,128)S(1)}, f32[3,28,1,1024]{3,2,1,0:T(1,128)S(1)}, u32[]{:S(2)}, u32[]{:S(2)}) collective-permute-start(f32[3,28,1,1024]{3,2,1,0:T(1,128)S(1)} %get-tuple-element.29), channel_id=1, source_target_pairs={{0,1},{1,2},{2,3},{3,4},{4,5},{5,6},{6,7},{7,0},{8,9},{9,10},{10,1... | collective-permute-start | bytes 1032200 | tf_op jit(solution)/shard_map/ppermute | solution.py:526
  10.3 2.6 %collective-permute-start.2 = (f32[3,28,1,1024]{3,2,1,0:T(1,128)S(1)}, f32[3,28,1,1024]{3,2,1,0:T(1,128)S(1)}, u32[]{:S(2)}, u32[]{:S(2)}) collective-permute-start(f32[3,28,1,1024]{3,2,1,0:T(1,128)S(1)} %get-tuple-element.30), channel_id=1, source_target_pairs={{1,0},{2,1},{3,2},{4,3},{5,4},{6,5},{7,6},{0,7},{9,8},{10,9},{11,1... | collective-permute-start | bytes 1032200 | tf_op jit(solution)/shard_map/ppermute | solution.py:527
  12.9 8.9 %inner_rows.1 = (f32[3,12,32,1024]{3,2,1,0:T(8,128)}, f32[3,16,32,1024]{3,2,1,0:T(8,128)}, f32[3,28,8,48,128]{4,3,2,1,0:T(8,128)S(1)}, f32[3,2,32,1024]{3,2,1,0:T(8,128)S(1)}, f32[3,2,32,1024]{3,2,1,0:T(8,128)S(1)}) custom-call(f32[3,12,32,1024]{3,2,1,0:T(8,128)} %refs_0_.4, f32[3,16,32,1024]{3,2,1,0:T(8,128)} %prec.1, f32[3,12,32,1024]{3,2,1,0:T(8,128)} %refs_1_.7), custom_call_target="tpu_custom_call" | custom-call | bytes 33300000 | tf_op jit(solution)/shard_map/inner_rows/pallas_call | solution.py:287
  21.8 0.0 collective-permute-done.3.refs_2_
  21.8 0.0 collective-permute-done.4.refs_3_
  21.8 0.0 collective-permute-done.5.refs_4_
  21.8 0.0 collective-permute-done.1.refs_2_
  21.8 5.2 %collective-permute-done.2.refs_3_ = f32[3,28,1,1024]{3,2,1,0:T(1,128)S(1)} collective-permute-done((f32[3,28,1,1024]{3,2,1,0:T(1,128)S(1)}, f32[3,28,1,1024]{3,2,1,0:T(1,128)S(1)}, u32[]{:S(2)}, u32[]{:S(2)}) %collective-permute-start.2) | collective-permute-done | bytes 344096 | tf_op jit(solution)/shard_map/ppermute | solution.py:527
  27.0 0.0 collective-permute-start.6
  27.0 8.0 %collective-permute-start.7 = (f32[3,2,32,1024]{3,2,1,0:T(8,128)S(1)}, f32[3,2,32,1024]{3,2,1,0:T(8,128)S(1)}, u32[]{:S(2)}, u32[]{:S(2)}) collective-permute-start(f32[3,2,32,1024]{3,2,1,0:T(8,128)S(1)} %get-tuple-element.35), channel_id=1, source_target_pairs={{8,0},{16,8},{24,16},{32,24},{40,32},{48,40},{56,48},{64,56},{72,6... | collective-permute-start | bytes 2359304 | tf_op jit(solution)/shard_map/ppermute | solution.py:531
  35.0 0.0 copy-done
  35.0 0.6 %relay_rows.1 = (f32[3,32,1024]{2,1,0:T(8,128)S(1)}, f32[3,32,1024]{2,1,0:T(8,128)S(1)}) custom-call(s32[256]{0:T(256)S(1)} %copy-done, f32[3,32,1024]{2,1,0:T(8,128)S(1)} %collective-permute-done.refs_1_, f32[3,32,1024]{2,1,0:T(8,128)S(1)} %collective-permute-done.3.refs_2_, f32[3,32,1024]{2,1,0:T(8,128)S(1)} %collective-permute-done.4.refs_3_, ...), custom_call_target="tpu_custom_call" | custom-call | bytes 3700000 | tf_op jit(solution)/shard_map/relay_rows/pallas_call | solution.py:490
  35.6 1.3 %collective-permute-start.8 = (f32[3,32,1024]{2,1,0:T(8,128)S(1)}, f32[3,32,1024]{2,1,0:T(8,128)S(1)}, u32[]{:S(2)}, u32[]{:S(2)}) collective-permute-start(f32[3,32,1024]{2,1,0:T(8,128)S(1)} %get-tuple-element.40), channel_id=1, source_target_pairs={{112,0},{113,1},{114,2},{115,3},{116,4},{117,5},{118,6},{119,7}} | collective-permute-start | bytes 1179656 | tf_op jit(solution)/shard_map/ppermute | solution.py:516
  36.9 1.3 %collective-permute-start.9 = (f32[3,32,1024]{2,1,0:T(8,128)S(1)}, f32[3,32,1024]{2,1,0:T(8,128)S(1)}, u32[]{:S(2)}, u32[]{:S(2)}) collective-permute-start(f32[3,32,1024]{2,1,0:T(8,128)S(1)} %get-tuple-element.41), channel_id=1, source_target_pairs={{112,1},{113,0},{114,3},{115,2},{116,5},{117,4},{118,7},{119,6}} | collective-permute-start | bytes 1179656 | tf_op jit(solution)/shard_map/ppermute | solution.py:516
  38.2 7.4 %edge_rows.1 = (f32[3,12,32,1024]{3,2,1,0:T(8,128)}, f32[3,16,32,1024]{3,2,1,0:T(8,128)}) custom-call(f32[3,28,8,48,128]{4,3,2,1,0:T(8,128)S(1)} %get-tuple-element.24.refs_0_, f32[3,12,32,1024]{3,2,1,0:T(8,128)} %refs_1_.7, f32[3,28,1,1024]{3,2,1,0:T(1,128)S(1)} %collective-permute-done.1.refs_2_, ...), custom_call_target="tpu_custom_call", output_to_operand_aliasing={{0}: (4, {}), {1}: (5, {})} | custom-call | bytes 29600000 | tf_op jit(solution)/shard_map/edge_rows/pallas_call | solution.py:287
  45.7 7.4 %collective-permute-done.8.refs_6_ = f32[3,32,1024]{2,1,0:T(8,128)S(1)} collective-permute-done((f32[3,32,1024]{2,1,0:T(8,128)S(1)}, f32[3,32,1024]{2,1,0:T(8,128)S(1)}, u32[]{:S(2)}, u32[]{:S(2)}) %collective-permute-start.8) | collective-permute-done | bytes 393248 | tf_op jit(solution)/shard_map/ppermute | solution.py:516
  53.1 0.0 collective-permute-done.9.refs_7_
  53.1 0.0 collective-permute-done.6.refs_4_
  53.1 0.0 collective-permute-done.7.refs_5_
  53.1 2.9 %end_planes.1 = (f32[3,12,32,1024]{3,2,1,0:T(8,128)}, f32[3,16,32,1024]{3,2,1,0:T(8,128)}) custom-call(f32[3,28,8,48,128]{4,3,2,1,0:T(8,128)S(1)} %get-tuple-element.24.refs_0_, f32[3,12,32,1024]{3,2,1,0:T(8,128)} %refs_1_.7, f32[3,28,1,1024]{3,2,1,0:T(1,128)S(1)} %collective-permute-done.1.refs_2_, ...), custom_call_target="tpu_custom_call", output_to_operand_aliasing={{0}: (8, {}), {1}: (9, {})} | custom-call | bytes 14800000 | tf_op jit(solution)/shard_map/end_planes/pallas_call | solution.py:356
Async XLA Ops:
  1.6 5.5 %collective-permute-start = (f32[3,32,1024]{2,1,0:T(8,128)S(1)}, f32[3,32,1024]{2,1,0:T(8,128)S(1)}, u32[]{:S(2)}, u32[]{:S(2)}) collective-permute-start(f32[3,32,1024]{2,1,0:T(8,128)S(1)} %outlet_plane.1), channel_id=1, source_target_pairs={{120,112},{121,113},{122,114},{123,115},{124,116},{125,117},{126,1... | collective-permute-start | bytes 1179656 | tf_op jit(solution)/shard_map/ppermute | solution.py:516
  2.3 19.5 %collective-permute-start.3 = (f32[3,32,1024]{2,1,0:T(8,128)S(1)}, f32[3,32,1024]{2,1,0:T(8,128)S(1)}, u32[]{:S(2)}, u32[]{:S(2)}) collective-permute-start(f32[3,32,1024]{2,1,0:T(8,128)S(1)} %outlet_plane.1), channel_id=1, source_target_pairs={{120,114},{121,115},{122,112},{123,113},{124,118},{125,119},{126,1... | collective-permute-start | bytes 1179656 | tf_op jit(solution)/shard_map/ppermute | solution.py:516
  3.0 18.8 %collective-permute-start.4 = (f32[3,32,1024]{2,1,0:T(8,128)S(1)}, f32[3,32,1024]{2,1,0:T(8,128)S(1)}, u32[]{:S(2)}, u32[]{:S(2)}) collective-permute-start(f32[3,32,1024]{2,1,0:T(8,128)S(1)} %outlet_plane.1), channel_id=1, source_target_pairs={{120,116},{121,117},{122,118},{123,119},{124,112},{125,113},{126,1... | collective-permute-start | bytes 1179656 | tf_op jit(solution)/shard_map/ppermute | solution.py:516
  3.7 18.1 %collective-permute-start.5 = (f32[3,32,1024]{2,1,0:T(8,128)S(1)}, f32[3,32,1024]{2,1,0:T(8,128)S(1)}, u32[]{:S(2)}, u32[]{:S(2)}) collective-permute-start(f32[3,32,1024]{2,1,0:T(8,128)S(1)} %outlet_plane.1), channel_id=1, source_target_pairs={{120,118},{121,119},{122,116},{123,117},{124,114},{125,115},{126,1... | collective-permute-start | bytes 1179656 | tf_op jit(solution)/shard_map/ppermute | solution.py:516
  7.2 27.8 %copy-start = (s32[256]{0:T(256)S(1)}, s32[256]{0:T(256)}, u32[]{:S(2)}) copy-start(s32[256]{0:T(256)} %refs_0_.5) | copy-start | bytes 3076
  7.2 14.6 %collective-permute-start.1 = (f32[3,28,1,1024]{3,2,1,0:T(1,128)S(1)}, f32[3,28,1,1024]{3,2,1,0:T(1,128)S(1)}, u32[]{:S(2)}, u32[]{:S(2)}) collective-permute-start(f32[3,28,1,1024]{3,2,1,0:T(1,128)S(1)} %get-tuple-element.29), channel_id=1, source_target_pairs={{0,1},{1,2},{2,3},{3,4},{4,5},{5,6},{6,7},{7,0},{8,9},{9,10},{10,1... | collective-permute-start | bytes 1032200 | tf_op jit(solution)/shard_map/ppermute | solution.py:526
  10.3 16.7 %collective-permute-start.2 = (f32[3,28,1,1024]{3,2,1,0:T(1,128)S(1)}, f32[3,28,1,1024]{3,2,1,0:T(1,128)S(1)}, u32[]{:S(2)}, u32[]{:S(2)}) collective-permute-start(f32[3,28,1,1024]{3,2,1,0:T(1,128)S(1)} %get-tuple-element.30), channel_id=1, source_target_pairs={{1,0},{2,1},{3,2},{4,3},{5,4},{6,5},{7,6},{0,7},{9,8},{10,9},{11,1... | collective-permute-start | bytes 1032200 | tf_op jit(solution)/shard_map/ppermute | solution.py:527
  27.0 26.1 %collective-permute-start.6 = (f32[3,2,32,1024]{3,2,1,0:T(8,128)S(1)}, f32[3,2,32,1024]{3,2,1,0:T(8,128)S(1)}, u32[]{:S(2)}, u32[]{:S(2)}) collective-permute-start(f32[3,2,32,1024]{3,2,1,0:T(8,128)S(1)} %get-tuple-element.34), channel_id=1, source_target_pairs={{0,8},{8,16},{16,24},{24,32},{32,40},{40,48},{48,56},{56,64},{64,7... | collective-permute-start | bytes 2359304 | tf_op jit(solution)/shard_map/ppermute | solution.py:530
  27.0 26.1 %collective-permute-start.7 = (f32[3,2,32,1024]{3,2,1,0:T(8,128)S(1)}, f32[3,2,32,1024]{3,2,1,0:T(8,128)S(1)}, u32[]{:S(2)}, u32[]{:S(2)}) collective-permute-start(f32[3,2,32,1024]{3,2,1,0:T(8,128)S(1)} %get-tuple-element.35), channel_id=1, source_target_pairs={{8,0},{16,8},{24,16},{32,24},{40,32},{48,40},{56,48},{64,56},{72,6... | collective-permute-start | bytes 2359304 | tf_op jit(solution)/shard_map/ppermute | solution.py:531
  35.6 17.5 %collective-permute-start.8 = (f32[3,32,1024]{2,1,0:T(8,128)S(1)}, f32[3,32,1024]{2,1,0:T(8,128)S(1)}, u32[]{:S(2)}, u32[]{:S(2)}) collective-permute-start(f32[3,32,1024]{2,1,0:T(8,128)S(1)} %get-tuple-element.40), channel_id=1, source_target_pairs={{112,0},{113,1},{114,2},{115,3},{116,4},{117,5},{118,6},{119,7}} | collective-permute-start | bytes 1179656 | tf_op jit(solution)/shard_map/ppermute | solution.py:516
  36.9 16.2 %collective-permute-start.9 = (f32[3,32,1024]{2,1,0:T(8,128)S(1)}, f32[3,32,1024]{2,1,0:T(8,128)S(1)}, u32[]{:S(2)}, u32[]{:S(2)}) collective-permute-start(f32[3,32,1024]{2,1,0:T(8,128)S(1)} %get-tuple-element.41), channel_id=1, source_target_pairs={{112,1},{113,0},{114,3},{115,2},{116,5},{117,4},{118,7},{119,6}} | collective-permute-start | bytes 1179656 | tf_op jit(solution)/shard_map/ppermute | solution.py:516

commit v2 on v1

--- a/solution.py
+++ b/solution.py
@@ -297,13 +297,12 @@
     )(*operands)
 
 
-def boundary_kernel(n_main, n_prec, rows, jobs, chunks, *refs):
-    flow, magnet, low, high, before, after = refs[:6]
-    slots = refs[6 : 6 + chunks]
-    main_out, prec_out, field, result, field_sem, out_sem = refs[8 + chunks :]
+def boundary_kernel(n_main, n_prec, rows, jobs, *refs):
+    flow, magnet, low, high, before, after, fed = refs[:7]
+    main_out, prec_out, field, result, field_sem, out_sem = refs[9:]
     last = rows // SUBLANES - 1
     tiles = flow.shape[2]
-    _, _, at_inlet, at_outlet = place()
+    at_outlet = place()[3]
     for job, (is_main, at_low) in enumerate(jobs):
         if is_main:
             x = 0 if at_low else n_main - 1
@@ -322,8 +321,7 @@
                 result[c, job, pl.ds(k * SUBLANES, SUBLANES), tile_of(t)] = value
 
             def inlet(c, t, k=k, face=face):
-                fed = span_rows(slots[0], c, t, k) + span_rows(slots[1], c, t, k)
-                return jnp.where(at_inlet, fed, face(c, t))
+                return face(c, t) + span_rows(fed, c, t, k)
 
             def outlet(c, t, center=center, face=face):
                 return jnp.where(at_outlet, center(c, t), face(c, t))
@@ -349,14 +347,13 @@
         wait_part(result.at[:, job], out_sem.at[job])
 
 
-def boundary(jobs, n_main, n_prec, flow, magnet, low, high, before, after, slots, main_out, prec_out):
+def boundary(jobs, n_main, n_prec, flow, magnet, low, high, before, after, fed, main_out, prec_out):
     _, _, rows, depth = magnet.shape
     count = len(jobs)
-    chunks = len(slots)
     return pl.pallas_call(
-        functools.partial(boundary_kernel, n_main, n_prec, rows, jobs, chunks),
+        functools.partial(boundary_kernel, n_main, n_prec, rows, jobs),
         out_shape=[jax.ShapeDtypeStruct(main_out.shape, F32), jax.ShapeDtypeStruct(prec_out.shape, F32)],
-        in_specs=[VMEM, HBM] + [VMEM] * (4 + chunks) + [HBM] * 2,
+        in_specs=[VMEM, HBM] + [VMEM] * 5 + [HBM] * 2,
         out_specs=[HBM, HBM],
         scratch_shapes=[
             pltpu.VMEM((3, count, rows, depth), F32),
@@ -364,11 +361,11 @@
             pltpu.SemaphoreType.DMA((count,)),
             pltpu.SemaphoreType.DMA((count,)),
         ],
-        input_output_aliases={6 + chunks: 0, 7 + chunks: 1},
+        input_output_aliases={7: 0, 8: 1},
         compiler_params=pltpu.CompilerParams(vmem_limit_bytes=8 << 20),
         cost_estimate=cost(len(jobs)),
         name="end_planes",
-    )(flow, magnet, low, high, before, after, *slots, main_out, prec_out)
+    )(flow, magnet, low, high, before, after, fed, main_out, prec_out)
 
 
 def outlet_kernel(prec, plane, sem):
@@ -446,62 +443,63 @@
 
 def relay_kernel(rows, *refs):
     order = refs[0]
-    sources = refs[1:-6]
-    outs = refs[-6:-4]
-    held, laid, sem, out_sem = refs[-4:]
+    sources = refs[1:-7]
+    face, theirs, held, laid, sem, out_sem = refs[-6:]
     span_index = lax.axis_index("span")
     tiles = held.shape[2]
 
-    @pl.when(lax.axis_index("stream") == lax.axis_size("stream") - 2)
+    @pl.when(place()[3])
     def _():
         for m, source in enumerate(sources):
             for t in range(tiles):
-                pltpu.make_async_copy(source.at[:, :, tile_of(t)], held.at[m, :, t], sem.at[m]).start()
-        laid[...] = jnp.zeros_like(laid)
+                pltpu.make_async_copy(
+                    source.at[:, :, tile_of(t)], held.at[m, :, t, pl.ds(0, rows)], sem.at[m]
+                ).start()
+        for c in range(3):
+            for t in range(tiles):
+                held[0, c, t, pl.ds(rows, SUBLANES), :] = jnp.zeros((SUBLANES, LANES), F32)
         for m in range(len(sources)):
-            wait_part(held.at[m], sem.at[m])
+            wait_part(held.at[m, :, :, pl.ds(0, rows)], sem.at[m])
         for k in range(2):
             base = jnp.bitwise_xor(span_index, k) * rows
 
             def step(r, carry, k=k, base=base):
                 row = order[base + r]
                 away = jnp.bitwise_xor(row // rows, span_index)
-                at = row % rows
-
-                @pl.when(away % 2 == 0)
-                def _():
-                    for c in range(3):
-                        for t in range(tiles):
-                            laid[k, c, t, pl.ds(r, 1), :] = held[away // 2, c, t, pl.ds(at, 1), :]
-
+                here = away % 2 == 0
+                m = jnp.where(here, away // 2, 0)
+                at = jnp.where(here, row % rows, rows)
+                for c in range(3):
+                    for t in range(tiles):
+                        laid[k, c, t, pl.ds(r, 1), :] = held[m, c, t, pl.ds(at, 1), :]
                 return carry
 
-            lax.fori_loop(0, rows, step, 0)
+            lax.fori_loop(0, rows, step, 0, unroll=4)
+            target = face.at[:, 0] if k == 0 else theirs
             for t in range(tiles):
-                pltpu.make_async_copy(laid.at[k, :, t], outs[k].at[:, :, tile_of(t)], out_sem.at[k]).start()
+                pltpu.make_async_copy(laid.at[k, :, t], target.at[:, :, tile_of(t)], out_sem.at[k]).start()
         for k in range(2):
             wait_part(laid.at[k], out_sem.at[k])
 
 
-def relay(order, sources):
+def relay(order, sources, face):
     _, rows, depth = sources[0].shape
-    piece = pltpu.VMEM((3, rows, depth), F32)
-    tiles = depth // LANES
     return pl.pallas_call(
         functools.partial(relay_kernel, rows),
-        out_shape=[piece] * 2,
-        in_specs=[SMEM] + [VMEM] * len(sources),
+        out_shape=[pltpu.VMEM(face.shape, F32), pltpu.VMEM((3, rows, depth), F32)],
+        in_specs=[SMEM] + [VMEM] * (len(sources) + 1),
         out_specs=[VMEM] * 2,
         scratch_shapes=[
-            pltpu.VMEM((len(sources), 3, tiles, rows, LANES), F32),
-            pltpu.VMEM((2, 3, tiles, rows, LANES), F32),
+            pltpu.VMEM((len(sources), 3, depth // LANES, rows + SUBLANES, LANES), F32),
+            pltpu.VMEM((2, 3, depth // LANES, rows, LANES), F32),
             pltpu.SemaphoreType.DMA((len(sources),)),
             pltpu.SemaphoreType.DMA((2,)),
         ],
+        input_output_aliases={len(sources) + 1: 0},
         compiler_params=pltpu.CompilerParams(vmem_limit_bytes=8 << 20),
         cost_estimate=cost(1),
         name="relay_rows",
-    )(order, *sources)
+    )(order, *sources, face)
 
 
 def shards(main, prec, magnet, inlet_rows):
@@ -518,22 +516,22 @@
         )
 
     plane = outlet(prec)
-    sources = [hop(plane, last, last - 1, 2 * m) for m in range(spans // 2)]
+    sources = [plane] + [hop(plane, last, last, 2 * m) for m in range(1, spans // 2)]
     row_low, row_high = pack(main, prec)
-    row_low, row_high, sources[0] = lax.optimization_barrier((row_low, row_high, sources[0]))
     up_span = [(i, (i + 1) % spans) for i in range(spans)]
     up_stream = [(i, (i + 1) % streams) for i in range(streams)]
     low = lax.ppermute(row_high, "span", up_span)
     high = lax.ppermute(row_low, "span", [(b, a) for a, b in up_span])
     *outs, flow, face_low, face_high = interior(False, main.shape, prec.shape, (main, prec, magnet))
-    face_low, face_high, low, high, *sources = lax.optimization_barrier((face_low, face_high, low, high, *sources))
+    face_low, face_high, *sources = lax.optimization_barrier((face_low, face_high, *sources))
+    face_high, theirs = relay(inlet_rows, sources, face_high)
+    face_low, face_high, low, high, theirs = lax.optimization_barrier((face_low, face_high, low, high, theirs))
+    fed = hop(theirs, last, 0, 1)
     before = lax.ppermute(face_high, "stream", up_stream)
     after = lax.ppermute(face_low, "stream", [(b, a) for a, b in up_stream])
-    laid = relay(inlet_rows, sources)
-    slots = [hop(laid[k], last - 1, 0, k) for k in range(2)]
     outs = interior(True, main.shape, prec.shape, (flow, magnet, low, high, *outs))
     ends = ((False, True), (False, False), (True, False), (True, True))
-    outs = boundary(ends, n_main, n_prec, flow, magnet, low, high, before, after, slots, *outs)
+    outs = boundary(ends, n_main, n_prec, flow, magnet, low, high, before, after, fed, *outs)
     return tuple(outs)
 
 

time: 56.2 us -> 52.1 us (0.927)
  waiting for transfers between devices: 12.6 us -> 9.61 us
  starting transfers between devices: 19 us -> 17.4 us
    ppermute x6 -> x4, waiting for transfers between devices: 7.44 us -> 5.08 us  [hop(): lax.ppermute(value, axes, [(source * spans + a, target * spans + (a ^ k))...]
    ppermute x6 -> x4, starting transfers between devices: 5.33 us -> 3.34 us  [hop(): lax.ppermute(value, axes, [(source * spans + a, target * spans + (a ^ k))...]
    ppermute x1, waiting for transfers between devices: 5.17 us -> 4.52 us  [shards(): high = lax.ppermute(row_low, 'span', [(b, a) for a, b in up_span])]
    pallas_call x1, Pallas kernels: 2.89 us -> 3.45 us  [boundary(): pl.pallas_call(functools.partial(boundary_kernel, n_main, n_prec, rows, j...]
  transfers between devices with their start and end apart: 10 -> 8, of which waited for: 2 -> 2; matrix products, arithmetic and copies ran while one was open for 0% -> 0% of each run, Pallas kernels for 35% -> 38%
where the time goes in v2:
time: 52.1 us; the launch traced here: 51.9 us
  Pallas kernels  24.1 us (46%)
  starting transfers between devices  17.4 us (33%)
  waiting for transfers between devices  9.61 us (18%)
  between operations  0.74 us (1%)
    pallas_call x2, Pallas kernels, interior(): pl.pallas_call(functools.partial(interior_kernel, edges, n_main, n_prec,...  16.3 us
    ppermute x1, starting transfers between devices, shards(): after = lax.ppermute(face_low, 'stream', [(b, a) for a, b in up_stream])  8.31 us
    ppermute x4, waiting for transfers between devices, hop(): lax.ppermute(value, axes, [(source * spans + a, target * spans + (a ^ k))...  5.08 us
    ppermute x1, waiting for transfers between devices, shards(): high = lax.ppermute(row_low, 'span', [(b, a) for a, b in up_span])  4.52 us
    pallas_call x1, Pallas kernels, boundary(): pl.pallas_call(functools.partial(boundary_kernel, n_main, n_prec, rows, j...  3.45 us
    ppermute x4, starting transfers between devices, hop(): lax.ppermute(value, axes, [(source * spans + a, target * spans + (a ^ k))...  3.34 us
    ppermute x1, starting transfers between devices, shards(): low = lax.ppermute(row_high, 'span', up_span)  3.16 us
    pallas_call x1, Pallas kernels, pack(): pl.pallas_call(functools.partial(pack_kernel, n_main, n_prec, rows), out_...  2.72 us
  transfers between devices with their start and end apart: 8, of which 2 were waited for; matrix products, arithmetic and copies ran while one was open for 0% of the time, Pallas kernels for 38%

profile of v2, /device:TPU:0, one launch (start us, length us, event | category | flops | bytes accessed | tf_op | source)
XLA Modules:
  0.0 51.9 jit_solution(1447997293607659806)
XLA Ops:
  0.6 1.0 %outlet_plane.1.refs_1_ = f32[3,32,1024]{2,1,0:T(8,128)S(1)} custom-call(f32[3,16,32,1024]{3,2,1,0:T(8,128)} %refs_1_.5), custom_call_target="tpu_custom_call" | custom-call | bytes 3700000 | tf_op jit(solution)/shard_map/outlet_plane/pallas_call | solution.py:379
  1.6 0.7 %collective-permute-start.2 = (f32[3,32,1024]{2,1,0:T(8,128)S(1)}, f32[3,32,1024]{2,1,0:T(8,128)S(1)}, u32[]{:S(2)}, u32[]{:S(2)}) collective-permute-start(f32[3,32,1024]{2,1,0:T(8,128)S(1)} %outlet_plane.1.refs_1_), channel_id=1, source_target_pairs={{120,126},{121,127},{122,124},{123,125},{124,122},{125,123},{126,1... | collective-permute-start | bytes 1179656 | tf_op jit(solution)/shard_map/ppermute | solution.py:514
  2.3 0.7 %collective-permute-start.1 = (f32[3,32,1024]{2,1,0:T(8,128)S(1)}, f32[3,32,1024]{2,1,0:T(8,128)S(1)}, u32[]{:S(2)}, u32[]{:S(2)}) collective-permute-start(f32[3,32,1024]{2,1,0:T(8,128)S(1)} %outlet_plane.1.refs_1_), channel_id=1, source_target_pairs={{120,124},{121,125},{122,126},{123,127},{124,120},{125,121},{126,1... | collective-permute-start | bytes 1179656 | tf_op jit(solution)/shard_map/ppermute | solution.py:514
  3.0 0.7 %collective-permute-start = (f32[3,32,1024]{2,1,0:T(8,128)S(1)}, f32[3,32,1024]{2,1,0:T(8,128)S(1)}, u32[]{:S(2)}, u32[]{:S(2)}) collective-permute-start(f32[3,32,1024]{2,1,0:T(8,128)S(1)} %outlet_plane.1.refs_1_), channel_id=1, source_target_pairs={{120,122},{121,123},{122,120},{123,121},{124,126},{125,127},{126,1... | collective-permute-start | bytes 1179656 | tf_op jit(solution)/shard_map/ppermute | solution.py:514
  3.7 2.7 %pack_rows.1 = (f32[3,28,1,1024]{3,2,1,0:T(1,128)S(1)}, f32[3,28,1,1024]{3,2,1,0:T(1,128)S(1)}) custom-call(f32[3,12,32,1024]{3,2,1,0:T(8,128)} %refs_0_.5, f32[3,16,32,1024]{3,2,1,0:T(8,128)} %refs_1_.5), custom_call_target="tpu_custom_call" | custom-call | bytes 11100000 | tf_op jit(solution)/shard_map/pack_rows/pallas_call | solution.py:428
  6.5 3.2 %collective-permute-start.3 = (f32[3,28,1,1024]{3,2,1,0:T(1,128)S(1)}, f32[3,28,1,1024]{3,2,1,0:T(1,128)S(1)}, u32[]{:S(2)}, u32[]{:S(2)}) collective-permute-start(f32[3,28,1,1024]{3,2,1,0:T(1,128)S(1)} %get-tuple-element.34), channel_id=1, source_target_pairs={{0,1},{1,2},{2,3},{3,4},{4,5},{5,6},{6,7},{7,0},{8,9},{9,10},{10,1... | collective-permute-start | bytes 1032200 | tf_op jit(solution)/shard_map/ppermute | solution.py:523
  9.6 0.0 copy-start
  9.6 2.6 %collective-permute-start.4 = (f32[3,28,1,1024]{3,2,1,0:T(1,128)S(1)}, f32[3,28,1,1024]{3,2,1,0:T(1,128)S(1)}, u32[]{:S(2)}, u32[]{:S(2)}) collective-permute-start(f32[3,28,1,1024]{3,2,1,0:T(1,128)S(1)} %get-tuple-element.35), channel_id=1, source_target_pairs={{1,0},{2,1},{3,2},{4,3},{5,4},{6,5},{7,6},{0,7},{9,8},{10,9},{11,1... | collective-permute-start | bytes 1032200 | tf_op jit(solution)/shard_map/ppermute | solution.py:524
  12.2 8.9 %inner_rows.1 = (f32[3,12,32,1024]{3,2,1,0:T(8,128)}, f32[3,16,32,1024]{3,2,1,0:T(8,128)}, f32[3,28,8,48,128]{4,3,2,1,0:T(8,128)S(1)}, f32[3,2,32,1024]{3,2,1,0:T(8,128)S(1)}, f32[3,2,32,1024]{3,2,1,0:T(8,128)S(1)}) custom-call(f32[3,12,32,1024]{3,2,1,0:T(8,128)} %refs_0_.5, f32[3,16,32,1024]{3,2,1,0:T(8,128)} %refs_1_.5, f32[3,12,32,1024]{3,2,1,0:T(8,128)} %refs_1_.7), custom_call_target="tpu_custom_call" | custom-call | bytes 33300000 | tf_op jit(solution)/shard_map/inner_rows/pallas_call | solution.py:287
  21.1 0.0 collective-permute-done.2.refs_4_
  21.1 0.0 collective-permute-done.1.refs_3_
  21.1 0.0 collective-permute-done.refs_2_
  21.1 0.0 copy-done
  21.1 0.6 %relay_rows.1 = (f32[3,2,32,1024]{3,2,1,0:T(8,128)S(1)}, f32[3,32,1024]{2,1,0:T(8,128)S(1)}) custom-call(s32[256]{0:T(256)S(1)} %copy-done, f32[3,32,1024]{2,1,0:T(8,128)S(1)} %outlet_plane.1.refs_1_, f32[3,32,1024]{2,1,0:T(8,128)S(1)} %collective-permute-done.refs_2_, ...), custom_call_target="tpu_custom_call", output_to_operand_aliasing={{0}: (5, {})} | custom-call | bytes 3700000 | tf_op jit(solution)/shard_map/relay_rows/pallas_call | solution.py:487
  21.8 0.0 collective-permute-done.3.refs_2_
  21.8 4.5 %collective-permute-done.4.refs_3_ = f32[3,28,1,1024]{3,2,1,0:T(1,128)S(1)} collective-permute-done((f32[3,28,1,1024]{3,2,1,0:T(1,128)S(1)}, f32[3,28,1,1024]{3,2,1,0:T(1,128)S(1)}, u32[]{:S(2)}, u32[]{:S(2)}) %collective-permute-start.4) | collective-permute-done | bytes 344096 | tf_op jit(solution)/shard_map/ppermute | solution.py:524
  26.3 0.0 collective-permute-start.5
  26.3 8.3 %collective-permute-start.6 = (f32[3,2,32,1024]{3,2,1,0:T(8,128)S(1)}, f32[3,2,32,1024]{3,2,1,0:T(8,128)S(1)}, u32[]{:S(2)}, u32[]{:S(2)}) collective-permute-start(f32[3,2,32,1024]{3,2,1,0:T(8,128)S(1)} %get-tuple-element.40), channel_id=1, source_target_pairs={{8,0},{16,8},{24,16},{32,24},{40,32},{48,40},{56,48},{64,56},{72,6... | collective-permute-start | bytes 2359304 | tf_op jit(solution)/shard_map/ppermute | solution.py:531
  34.6 1.3 %collective-permute-start.7 = (f32[3,32,1024]{2,1,0:T(8,128)S(1)}, f32[3,32,1024]{2,1,0:T(8,128)S(1)}, u32[]{:S(2)}, u32[]{:S(2)}) collective-permute-start(f32[3,32,1024]{2,1,0:T(8,128)S(1)} %get-tuple-element.41), channel_id=1, source_target_pairs={{120,1},{121,0},{122,3},{123,2},{124,5},{125,4},{126,7},{127,6}} | collective-permute-start | bytes 1179656 | tf_op jit(solution)/shard_map/ppermute | solution.py:514
  35.9 7.4 %edge_rows.1 = (f32[3,12,32,1024]{3,2,1,0:T(8,128)}, f32[3,16,32,1024]{3,2,1,0:T(8,128)}) custom-call(f32[3,28,8,48,128]{4,3,2,1,0:T(8,128)S(1)} %get-tuple-element.24.refs_0_, f32[3,12,32,1024]{3,2,1,0:T(8,128)} %refs_1_.7, f32[3,28,1,1024]{3,2,1,0:T(1,128)S(1)} %collective-permute-done.3.refs_2_, ...), custom_call_target="tpu_custom_call", output_to_operand_aliasing={{0}: (4, {}), {1}: (5, {})} | custom-call | bytes 29600000 | tf_op jit(solution)/shard_map/edge_rows/pallas_call | solution.py:287
  43.3 5.1 %collective-permute-done.7.refs_6_ = f32[3,32,1024]{2,1,0:T(8,128)S(1)} collective-permute-done((f32[3,32,1024]{2,1,0:T(8,128)S(1)}, f32[3,32,1024]{2,1,0:T(8,128)S(1)}, u32[]{:S(2)}, u32[]{:S(2)}) %collective-permute-start.7) | collective-permute-done | bytes 393248 | tf_op jit(solution)/shard_map/ppermute | solution.py:514
  48.4 0.0 collective-permute-done.5.refs_4_
  48.4 0.0 collective-permute-done.6.refs_5_
  48.4 3.5 %end_planes.1 = (f32[3,12,32,1024]{3,2,1,0:T(8,128)}, f32[3,16,32,1024]{3,2,1,0:T(8,128)}) custom-call(f32[3,28,8,48,128]{4,3,2,1,0:T(8,128)S(1)} %get-tuple-element.24.refs_0_, f32[3,12,32,1024]{3,2,1,0:T(8,128)} %refs_1_.7, f32[3,28,1,1024]{3,2,1,0:T(1,128)S(1)} %collective-permute-done.3.refs_2_, ...), custom_call_target="tpu_custom_call", output_to_operand_aliasing={{0}: (7, {}), {1}: (8, {})} | custom-call | bytes 14800000 | tf_op jit(solution)/shard_map/end_planes/pallas_call | solution.py:353
Async XLA Ops:
  1.6 19.4 %collective-permute-start.2 = (f32[3,32,1024]{2,1,0:T(8,128)S(1)}, f32[3,32,1024]{2,1,0:T(8,128)S(1)}, u32[]{:S(2)}, u32[]{:S(2)}) collective-permute-start(f32[3,32,1024]{2,1,0:T(8,128)S(1)} %outlet_plane.1.refs_1_), channel_id=1, source_target_pairs={{120,126},{121,127},{122,124},{123,125},{124,122},{125,123},{126,1... | collective-permute-start | bytes 1179656 | tf_op jit(solution)/shard_map/ppermute | solution.py:514
  2.3 18.8 %collective-permute-start.1 = (f32[3,32,1024]{2,1,0:T(8,128)S(1)}, f32[3,32,1024]{2,1,0:T(8,128)S(1)}, u32[]{:S(2)}, u32[]{:S(2)}) collective-permute-start(f32[3,32,1024]{2,1,0:T(8,128)S(1)} %outlet_plane.1.refs_1_), channel_id=1, source_target_pairs={{120,124},{121,125},{122,126},{123,127},{124,120},{125,121},{126,1... | collective-permute-start | bytes 1179656 | tf_op jit(solution)/shard_map/ppermute | solution.py:514
  3.0 18.1 %collective-permute-start = (f32[3,32,1024]{2,1,0:T(8,128)S(1)}, f32[3,32,1024]{2,1,0:T(8,128)S(1)}, u32[]{:S(2)}, u32[]{:S(2)}) collective-permute-start(f32[3,32,1024]{2,1,0:T(8,128)S(1)} %outlet_plane.1.refs_1_), channel_id=1, source_target_pairs={{120,122},{121,123},{122,120},{123,121},{124,126},{125,127},{126,1... | collective-permute-start | bytes 1179656 | tf_op jit(solution)/shard_map/ppermute | solution.py:514
  6.5 15.3 %collective-permute-start.3 = (f32[3,28,1,1024]{3,2,1,0:T(1,128)S(1)}, f32[3,28,1,1024]{3,2,1,0:T(1,128)S(1)}, u32[]{:S(2)}, u32[]{:S(2)}) collective-permute-start(f32[3,28,1,1024]{3,2,1,0:T(1,128)S(1)} %get-tuple-element.34), channel_id=1, source_target_pairs={{0,1},{1,2},{2,3},{3,4},{4,5},{5,6},{6,7},{7,0},{8,9},{9,10},{10,1... | collective-permute-start | bytes 1032200 | tf_op jit(solution)/shard_map/ppermute | solution.py:523
  9.6 11.5 %copy-start = (s32[256]{0:T(256)S(1)}, s32[256]{0:T(256)}, u32[]{:S(2)}) copy-start(s32[256]{0:T(256)} %refs_0_.4) | copy-start | bytes 3076
  9.6 16.7 %collective-permute-start.4 = (f32[3,28,1,1024]{3,2,1,0:T(1,128)S(1)}, f32[3,28,1,1024]{3,2,1,0:T(1,128)S(1)}, u32[]{:S(2)}, u32[]{:S(2)}) collective-permute-start(f32[3,28,1,1024]{3,2,1,0:T(1,128)S(1)} %get-tuple-element.35), channel_id=1, source_target_pairs={{1,0},{2,1},{3,2},{4,3},{5,4},{6,5},{7,6},{0,7},{9,8},{10,9},{11,1... | collective-permute-start | bytes 1032200 | tf_op jit(solution)/shard_map/ppermute | solution.py:524
  26.3 22.1 %collective-permute-start.5 = (f32[3,2,32,1024]{3,2,1,0:T(8,128)S(1)}, f32[3,2,32,1024]{3,2,1,0:T(8,128)S(1)}, u32[]{:S(2)}, u32[]{:S(2)}) collective-permute-start(f32[3,2,32,1024]{3,2,1,0:T(8,128)S(1)} %get-tuple-element.39), channel_id=1, source_target_pairs={{0,8},{8,16},{16,24},{24,32},{32,40},{40,48},{48,56},{56,64},{64,7... | collective-permute-start | bytes 2359304 | tf_op jit(solution)/shard_map/ppermute | solution.py:530
  26.3 22.1 %collective-permute-start.6 = (f32[3,2,32,1024]{3,2,1,0:T(8,128)S(1)}, f32[3,2,32,1024]{3,2,1,0:T(8,128)S(1)}, u32[]{:S(2)}, u32[]{:S(2)}) collective-permute-start(f32[3,2,32,1024]{3,2,1,0:T(8,128)S(1)} %get-tuple-element.40), channel_id=1, source_target_pairs={{8,0},{16,8},{24,16},{32,24},{40,32},{48,40},{56,48},{64,56},{72,6... | collective-permute-start | bytes 2359304 | tf_op jit(solution)/shard_map/ppermute | solution.py:531
  34.6 13.8 %collective-permute-start.7 = (f32[3,32,1024]{2,1,0:T(8,128)S(1)}, f32[3,32,1024]{2,1,0:T(8,128)S(1)}, u32[]{:S(2)}, u32[]{:S(2)}) collective-permute-start(f32[3,32,1024]{2,1,0:T(8,128)S(1)} %get-tuple-element.41), channel_id=1, source_target_pairs={{120,1},{121,0},{122,3},{123,2},{124,5},{125,4},{126,7},{127,6}} | collective-permute-start | bytes 1179656 | tf_op jit(solution)/shard_map/ppermute | solution.py:514

commit v3 on v2

--- a/solution.py
+++ b/solution.py
@@ -297,9 +297,10 @@
     )(*operands)
 
 
-def boundary_kernel(n_main, n_prec, rows, jobs, *refs):
-    flow, magnet, low, high, before, after, fed = refs[:7]
-    main_out, prec_out, field, result, field_sem, out_sem = refs[9:]
+def boundary_kernel(n_main, n_prec, rows, jobs, parts, *refs):
+    flow, magnet, low, high, before, after = refs[:6]
+    inflow = refs[6 : 6 + parts]
+    main_out, prec_out, field, result, field_sem, out_sem = refs[8 + parts :]
     last = rows // SUBLANES - 1
     tiles = flow.shape[2]
     at_outlet = place()[3]
@@ -321,7 +322,7 @@
                 result[c, job, pl.ds(k * SUBLANES, SUBLANES), tile_of(t)] = value
 
             def inlet(c, t, k=k, face=face):
-                return face(c, t) + span_rows(fed, c, t, k)
+                return face(c, t) + span_rows(inflow[0], c, t, k)
 
             def outlet(c, t, center=center, face=face):
                 return jnp.where(at_outlet, center(c, t), face(c, t))
@@ -347,13 +348,13 @@
         wait_part(result.at[:, job], out_sem.at[job])
 
 
-def boundary(jobs, n_main, n_prec, flow, magnet, low, high, before, after, fed, main_out, prec_out):
+def boundary(jobs, n_main, n_prec, flow, magnet, low, high, before, after, inflow, main_out, prec_out):
     _, _, rows, depth = magnet.shape
     count = len(jobs)
     return pl.pallas_call(
-        functools.partial(boundary_kernel, n_main, n_prec, rows, jobs),
+        functools.partial(boundary_kernel, n_main, n_prec, rows, jobs, len(inflow)),
         out_shape=[jax.ShapeDtypeStruct(main_out.shape, F32), jax.ShapeDtypeStruct(prec_out.shape, F32)],
-        in_specs=[VMEM, HBM] + [VMEM] * 5 + [HBM] * 2,
+        in_specs=[VMEM, HBM] + [VMEM] * (4 + len(inflow)) + [HBM] * 2,
         out_specs=[HBM, HBM],
         scratch_shapes=[
             pltpu.VMEM((3, count, rows, depth), F32),
@@ -361,11 +362,11 @@
             pltpu.SemaphoreType.DMA((count,)),
             pltpu.SemaphoreType.DMA((count,)),
         ],
-        input_output_aliases={7: 0, 8: 1},
+        input_output_aliases={6 + len(inflow): 0, 7 + len(inflow): 1},
         compiler_params=pltpu.CompilerParams(vmem_limit_bytes=8 << 20),
         cost_estimate=cost(len(jobs)),
-        name="end_planes",
-    )(flow, magnet, low, high, before, after, fed, main_out, prec_out)
+        name="end_planes" if count > 1 else "inlet_plane",
+    )(flow, magnet, low, high, before, after, *inflow, main_out, prec_out)
 
 
 def outlet_kernel(prec, plane, sem):
@@ -530,8 +531,9 @@
     before = lax.ppermute(face_high, "stream", up_stream)
     after = lax.ppermute(face_low, "stream", [(b, a) for a, b in up_stream])
     outs = interior(True, main.shape, prec.shape, (flow, magnet, low, high, *outs))
-    ends = ((False, True), (False, False), (True, False), (True, True))
-    outs = boundary(ends, n_main, n_prec, flow, magnet, low, high, before, after, fed, *outs)
+    ends = ((False, True), (False, False), (True, False))
+    outs = boundary(ends, n_main, n_prec, flow, magnet, low, high, before, after, (), *outs)
+    outs = boundary(((True, True),), n_main, n_prec, flow, magnet, low, high, before, after, (fed,), *outs)
     return tuple(outs)
 
 

time: 52.1 us -> 51 us (0.979)
  waiting for transfers between devices: 9.61 us -> 7.26 us
  Pallas kernels: 24.1 us -> 25.3 us
    ppermute x4, waiting for transfers between devices: 5.08 us -> 0.08 us  [hop(): lax.ppermute(value, axes, [(source * spans + a, target * spans + (a ^ k))...]
    ppermute x1, waiting for transfers between devices: 0.01 us -> 2.65 us  [shards(): before = lax.ppermute(face_high, 'stream', up_stream)]
    pallas_call x1 -> x2, Pallas kernels: 3.45 us -> 4.61 us  [boundary(): pl.pallas_call(functools.partial(boundary_kernel, n_main, n_prec, rows, j...]
  transfers between devices with their start and end apart: 8 -> 8, of which waited for: 2 -> 3; matrix products, arithmetic and copies ran while one was open for 0% -> 0% of each run, Pallas kernels for 38% -> 43%
where the time goes in v3:
time: 51 us; the launch traced here: 50.7 us
  Pallas kernels  25.3 us (50%)
  starting transfers between devices  17.4 us (34%)
  waiting for transfers between devices  7.26 us (14%)
  between operations  0.75 us (1%)
    pallas_call x2, Pallas kernels, interior(): pl.pallas_call(functools.partial(interior_kernel, edges, n_main, n_prec,...  16.3 us
    ppermute x1, starting transfers between devices, shards(): after = lax.ppermute(face_low, 'stream', [(b, a) for a, b in up_stream])  8.31 us
    pallas_call x2, Pallas kernels, boundary(): pl.pallas_call(functools.partial(boundary_kernel, n_main, n_prec, rows, j...  4.61 us
    ppermute x1, waiting for transfers between devices, shards(): high = lax.ppermute(row_low, 'span', [(b, a) for a, b in up_span])  4.52 us
    ppermute x4, starting transfers between devices, hop(): lax.ppermute(value, axes, [(source * spans + a, target * spans + (a ^ k))...  3.34 us
    ppermute x1, starting transfers between devices, shards(): low = lax.ppermute(row_high, 'span', up_span)  3.16 us
    pallas_call x1, Pallas kernels, pack(): pl.pallas_call(functools.partial(pack_kernel, n_main, n_prec, rows), out_...  2.72 us
    ppermute x1, waiting for transfers between devices, shards(): before = lax.ppermute(face_high, 'stream', up_stream)  2.65 us
  transfers between devices with their start and end apart: 8, of which 3 were waited for; matrix products, arithmetic and copies ran while one was open for 0% of the time, Pallas kernels for 43%

profile of v3, /device:TPU:0, one launch (start us, length us, event | category | flops | bytes accessed | tf_op | source)
XLA Modules:
  0.0 50.7 jit_solution(2628020983239021042)
XLA Ops:
  0.6 1.0 %outlet_plane.1.refs_1_ = f32[3,32,1024]{2,1,0:T(8,128)S(1)} custom-call(f32[3,16,32,1024]{3,2,1,0:T(8,128)} %refs_1_.6), custom_call_target="tpu_custom_call" | custom-call | bytes 3700000 | tf_op jit(solution)/shard_map/outlet_plane/pallas_call | solution.py:380
  1.6 0.7 %collective-permute-start.2 = (f32[3,32,1024]{2,1,0:T(8,128)S(1)}, f32[3,32,1024]{2,1,0:T(8,128)S(1)}, u32[]{:S(2)}, u32[]{:S(2)}) collective-permute-start(f32[3,32,1024]{2,1,0:T(8,128)S(1)} %outlet_plane.1.refs_1_), channel_id=1, source_target_pairs={{120,126},{121,127},{122,124},{123,125},{124,122},{125,123},{126,1... | collective-permute-start | bytes 1179656 | tf_op jit(solution)/shard_map/ppermute | solution.py:515
  2.3 0.7 %collective-permute-start.1 = (f32[3,32,1024]{2,1,0:T(8,128)S(1)}, f32[3,32,1024]{2,1,0:T(8,128)S(1)}, u32[]{:S(2)}, u32[]{:S(2)}) collective-permute-start(f32[3,32,1024]{2,1,0:T(8,128)S(1)} %outlet_plane.1.refs_1_), channel_id=1, source_target_pairs={{120,124},{121,125},{122,126},{123,127},{124,120},{125,121},{126,1... | collective-permute-start | bytes 1179656 | tf_op jit(solution)/shard_map/ppermute | solution.py:515
  3.0 0.7 %collective-permute-start = (f32[3,32,1024]{2,1,0:T(8,128)S(1)}, f32[3,32,1024]{2,1,0:T(8,128)S(1)}, u32[]{:S(2)}, u32[]{:S(2)}) collective-permute-start(f32[3,32,1024]{2,1,0:T(8,128)S(1)} %outlet_plane.1.refs_1_), channel_id=1, source_target_pairs={{120,122},{121,123},{122,120},{123,121},{124,126},{125,127},{126,1... | collective-permute-start | bytes 1179656 | tf_op jit(solution)/shard_map/ppermute | solution.py:515
  3.7 2.7 %pack_rows.1 = (f32[3,28,1,1024]{3,2,1,0:T(1,128)S(1)}, f32[3,28,1,1024]{3,2,1,0:T(1,128)S(1)}) custom-call(f32[3,12,32,1024]{3,2,1,0:T(8,128)} %refs_0_.5, f32[3,16,32,1024]{3,2,1,0:T(8,128)} %refs_1_.6), custom_call_target="tpu_custom_call" | custom-call | bytes 11100000 | tf_op jit(solution)/shard_map/pack_rows/pallas_call | solution.py:429
  6.5 3.2 %collective-permute-start.3 = (f32[3,28,1,1024]{3,2,1,0:T(1,128)S(1)}, f32[3,28,1,1024]{3,2,1,0:T(1,128)S(1)}, u32[]{:S(2)}, u32[]{:S(2)}) collective-permute-start(f32[3,28,1,1024]{3,2,1,0:T(1,128)S(1)} %get-tuple-element.36), channel_id=1, source_target_pairs={{0,1},{1,2},{2,3},{3,4},{4,5},{5,6},{6,7},{7,0},{8,9},{9,10},{10,1... | collective-permute-start | bytes 1032200 | tf_op jit(solution)/shard_map/ppermute | solution.py:524
  9.6 0.0 copy-start
  9.6 2.6 %collective-permute-start.4 = (f32[3,28,1,1024]{3,2,1,0:T(1,128)S(1)}, f32[3,28,1,1024]{3,2,1,0:T(1,128)S(1)}, u32[]{:S(2)}, u32[]{:S(2)}) collective-permute-start(f32[3,28,1,1024]{3,2,1,0:T(1,128)S(1)} %get-tuple-element.37), channel_id=1, source_target_pairs={{1,0},{2,1},{3,2},{4,3},{5,4},{6,5},{7,6},{0,7},{9,8},{10,9},{11,1... | collective-permute-start | bytes 1032200 | tf_op jit(solution)/shard_map/ppermute | solution.py:525
  12.2 8.9 %inner_rows.1 = (f32[3,12,32,1024]{3,2,1,0:T(8,128)}, f32[3,16,32,1024]{3,2,1,0:T(8,128)}, f32[3,28,8,48,128]{4,3,2,1,0:T(8,128)S(1)}, f32[3,2,32,1024]{3,2,1,0:T(8,128)S(1)}, f32[3,2,32,1024]{3,2,1,0:T(8,128)S(1)}) custom-call(f32[3,12,32,1024]{3,2,1,0:T(8,128)} %refs_0_.5, f32[3,16,32,1024]{3,2,1,0:T(8,128)} %refs_1_.6, f32[3,12,32,1024]{3,2,1,0:T(8,128)} %refs_1_.9), custom_call_target="tpu_custom_call" | custom-call | bytes 33300000 | tf_op jit(solution)/shard_map/inner_rows/pallas_call | solution.py:287
  21.1 0.0 collective-permute-done.2.refs_4_
  21.1 0.0 collective-permute-done.1.refs_3_
  21.1 0.0 collective-permute-done.refs_2_
  21.1 0.0 copy-done
  21.1 0.6 %relay_rows.1 = (f32[3,2,32,1024]{3,2,1,0:T(8,128)S(1)}, f32[3,32,1024]{2,1,0:T(8,128)S(1)}) custom-call(s32[256]{0:T(256)S(1)} %copy-done, f32[3,32,1024]{2,1,0:T(8,128)S(1)} %outlet_plane.1.refs_1_, f32[3,32,1024]{2,1,0:T(8,128)S(1)} %collective-permute-done.refs_2_, ...), custom_call_target="tpu_custom_call", output_to_operand_aliasing={{0}: (5, {})} | custom-call | bytes 3700000 | tf_op jit(solution)/shard_map/relay_rows/pallas_call | solution.py:488
  21.8 0.0 collective-permute-done.3.refs_2_
  21.8 4.5 %collective-permute-done.4.refs_3_ = f32[3,28,1,1024]{3,2,1,0:T(1,128)S(1)} collective-permute-done((f32[3,28,1,1024]{3,2,1,0:T(1,128)S(1)}, f32[3,28,1,1024]{3,2,1,0:T(1,128)S(1)}, u32[]{:S(2)}, u32[]{:S(2)}) %collective-permute-start.4) | collective-permute-done | bytes 344096 | tf_op jit(solution)/shard_map/ppermute | solution.py:525
  26.3 0.0 collective-permute-start.5
  26.3 8.3 %collective-permute-start.6 = (f32[3,2,32,1024]{3,2,1,0:T(8,128)S(1)}, f32[3,2,32,1024]{3,2,1,0:T(8,128)S(1)}, u32[]{:S(2)}, u32[]{:S(2)}) collective-permute-start(f32[3,2,32,1024]{3,2,1,0:T(8,128)S(1)} %get-tuple-element.42), channel_id=1, source_target_pairs={{8,0},{16,8},{24,16},{32,24},{40,32},{48,40},{56,48},{64,56},{72,6... | collective-permute-start | bytes 2359304 | tf_op jit(solution)/shard_map/ppermute | solution.py:532
  34.6 1.3 %collective-permute-start.7 = (f32[3,32,1024]{2,1,0:T(8,128)S(1)}, f32[3,32,1024]{2,1,0:T(8,128)S(1)}, u32[]{:S(2)}, u32[]{:S(2)}) collective-permute-start(f32[3,32,1024]{2,1,0:T(8,128)S(1)} %get-tuple-element.43), channel_id=1, source_target_pairs={{120,1},{121,0},{122,3},{123,2},{124,5},{125,4},{126,7},{127,6}} | collective-permute-start | bytes 1179656 | tf_op jit(solution)/shard_map/ppermute | solution.py:515
  35.9 7.4 %edge_rows.1 = (f32[3,12,32,1024]{3,2,1,0:T(8,128)}, f32[3,16,32,1024]{3,2,1,0:T(8,128)}) custom-call(f32[3,28,8,48,128]{4,3,2,1,0:T(8,128)S(1)} %get-tuple-element.26.refs_0_, f32[3,12,32,1024]{3,2,1,0:T(8,128)} %refs_1_.9, f32[3,28,1,1024]{3,2,1,0:T(1,128)S(1)} %collective-permute-done.3.refs_2_, ...), custom_call_target="tpu_custom_call", output_to_operand_aliasing={{0}: (4, {}), {1}: (5, {})} | custom-call | bytes 29600000 | tf_op jit(solution)/shard_map/edge_rows/pallas_call | solution.py:287
  43.3 2.7 %collective-permute-done.5.refs_4_ = f32[3,2,32,1024]{3,2,1,0:T(8,128)S(1)} collective-permute-done((f32[3,2,32,1024]{3,2,1,0:T(8,128)S(1)}, f32[3,2,32,1024]{3,2,1,0:T(8,128)S(1)}, u32[]{:S(2)}, u32[]{:S(2)}) %collective-permute-start.5) | collective-permute-done | bytes 786464 | tf_op jit(solution)/shard_map/ppermute | solution.py:531
  46.0 0.0 collective-permute-done.6.refs_5_
  46.0 2.3 %end_planes.1 = (f32[3,12,32,1024]{3,2,1,0:T(8,128)}, f32[3,16,32,1024]{3,2,1,0:T(8,128)}) custom-call(f32[3,28,8,48,128]{4,3,2,1,0:T(8,128)S(1)} %get-tuple-element.26.refs_0_, f32[3,12,32,1024]{3,2,1,0:T(8,128)} %refs_1_.9, f32[3,28,1,1024]{3,2,1,0:T(1,128)S(1)} %collective-permute-done.3.refs_2_, ...), custom_call_target="tpu_custom_call", output_to_operand_aliasing={{0}: (6, {}), {1}: (7, {})} | custom-call | bytes 11100000 | tf_op jit(solution)/shard_map/end_planes/pallas_call | solution.py:354
  48.3 0.1 collective-permute-done.7.refs_6_
  48.4 2.3 %inlet_plane.1 = (f32[3,12,32,1024]{3,2,1,0:T(8,128)}, f32[3,16,32,1024]{3,2,1,0:T(8,128)}) custom-call(f32[3,28,8,48,128]{4,3,2,1,0:T(8,128)S(1)} %get-tuple-element.26.refs_0_, f32[3,12,32,1024]{3,2,1,0:T(8,128)} %refs_1_.9, f32[3,28,1,1024]{3,2,1,0:T(1,128)S(1)} %collective-permute-done.3.refs_2_, ...), custom_call_target="tpu_custom_call", output_to_operand_aliasing={{0}: (7, {}), {1}: (8, {})} | custom-call | bytes 3700000 | tf_op jit(solution)/shard_map/inlet_plane/pallas_call | solution.py:354
Async XLA Ops:
  1.6 19.4 %collective-permute-start.2 = (f32[3,32,1024]{2,1,0:T(8,128)S(1)}, f32[3,32,1024]{2,1,0:T(8,128)S(1)}, u32[]{:S(2)}, u32[]{:S(2)}) collective-permute-start(f32[3,32,1024]{2,1,0:T(8,128)S(1)} %outlet_plane.1.refs_1_), channel_id=1, source_target_pairs={{120,126},{121,127},{122,124},{123,125},{124,122},{125,123},{126,1... | collective-permute-start | bytes 1179656 | tf_op jit(solution)/shard_map/ppermute | solution.py:515
  2.3 18.8 %collective-permute-start.1 = (f32[3,32,1024]{2,1,0:T(8,128)S(1)}, f32[3,32,1024]{2,1,0:T(8,128)S(1)}, u32[]{:S(2)}, u32[]{:S(2)}) collective-permute-start(f32[3,32,1024]{2,1,0:T(8,128)S(1)} %outlet_plane.1.refs_1_), channel_id=1, source_target_pairs={{120,124},{121,125},{122,126},{123,127},{124,120},{125,121},{126,1... | collective-permute-start | bytes 1179656 | tf_op jit(solution)/shard_map/ppermute | solution.py:515
  3.0 18.1 %collective-permute-start = (f32[3,32,1024]{2,1,0:T(8,128)S(1)}, f32[3,32,1024]{2,1,0:T(8,128)S(1)}, u32[]{:S(2)}, u32[]{:S(2)}) collective-permute-start(f32[3,32,1024]{2,1,0:T(8,128)S(1)} %outlet_plane.1.refs_1_), channel_id=1, source_target_pairs={{120,122},{121,123},{122,120},{123,121},{124,126},{125,127},{126,1... | collective-permute-start | bytes 1179656 | tf_op jit(solution)/shard_map/ppermute | solution.py:515
  6.5 15.3 %collective-permute-start.3 = (f32[3,28,1,1024]{3,2,1,0:T(1,128)S(1)}, f32[3,28,1,1024]{3,2,1,0:T(1,128)S(1)}, u32[]{:S(2)}, u32[]{:S(2)}) collective-permute-start(f32[3,28,1,1024]{3,2,1,0:T(1,128)S(1)} %get-tuple-element.36), channel_id=1, source_target_pairs={{0,1},{1,2},{2,3},{3,4},{4,5},{5,6},{6,7},{7,0},{8,9},{9,10},{10,1... | collective-permute-start | bytes 1032200 | tf_op jit(solution)/shard_map/ppermute | solution.py:524
  9.6 11.5 %copy-start = (s32[256]{0:T(256)S(1)}, s32[256]{0:T(256)}, u32[]{:S(2)}) copy-start(s32[256]{0:T(256)} %refs_0_.4) | copy-start | bytes 3076
  9.6 16.7 %collective-permute-start.4 = (f32[3,28,1,1024]{3,2,1,0:T(1,128)S(1)}, f32[3,28,1,1024]{3,2,1,0:T(1,128)S(1)}, u32[]{:S(2)}, u32[]{:S(2)}) collective-permute-start(f32[3,28,1,1024]{3,2,1,0:T(1,128)S(1)} %get-tuple-element.37), channel_id=1, source_target_pairs={{1,0},{2,1},{3,2},{4,3},{5,4},{6,5},{7,6},{0,7},{9,8},{10,9},{11,1... | collective-permute-start | bytes 1032200 | tf_op jit(solution)/shard_map/ppermute | solution.py:525
  26.3 19.7 %collective-permute-start.5 = (f32[3,2,32,1024]{3,2,1,0:T(8,128)S(1)}, f32[3,2,32,1024]{3,2,1,0:T(8,128)S(1)}, u32[]{:S(2)}, u32[]{:S(2)}) collective-permute-start(f32[3,2,32,1024]{3,2,1,0:T(8,128)S(1)} %get-tuple-element.41), channel_id=1, source_target_pairs={{0,8},{8,16},{16,24},{24,32},{32,40},{40,48},{48,56},{56,64},{64,7... | collective-permute-start | bytes 2359304 | tf_op jit(solution)/shard_map/ppermute | solution.py:531
  26.3 19.7 %collective-permute-start.6 = (f32[3,2,32,1024]{3,2,1,0:T(8,128)S(1)}, f32[3,2,32,1024]{3,2,1,0:T(8,128)S(1)}, u32[]{:S(2)}, u32[]{:S(2)}) collective-permute-start(f32[3,2,32,1024]{3,2,1,0:T(8,128)S(1)} %get-tuple-element.42), channel_id=1, source_target_pairs={{8,0},{16,8},{24,16},{32,24},{40,32},{48,40},{56,48},{64,56},{72,6... | collective-permute-start | bytes 2359304 | tf_op jit(solution)/shard_map/ppermute | solution.py:532
  34.6 13.8 %collective-permute-start.7 = (f32[3,32,1024]{2,1,0:T(8,128)S(1)}, f32[3,32,1024]{2,1,0:T(8,128)S(1)}, u32[]{:S(2)}, u32[]{:S(2)}) collective-permute-start(f32[3,32,1024]{2,1,0:T(8,128)S(1)} %get-tuple-element.43), channel_id=1, source_target_pairs={{120,1},{121,0},{122,3},{123,2},{124,5},{125,4},{126,7},{127,6}} | collective-permute-start | bytes 1179656 | tf_op jit(solution)/shard_map/ppermute | solution.py:515
